TPU v7x, 512 devices: a whole 4x8x8 slice. The times are simulated.
512 devices in a mesh: replica: 16 (over x, z_hi), fsdp: 32 (over z_lo, y, core).
Axes of the slice: x: 4, y: 8, z: 8 (z_hi: 4, z_lo: 2; z = z_hi * 2 + z_lo), core: 2. Of those that a mesh axis runs over, the one named last changes fastest.
Arguments:
- anchor: float32 [3328, 3328], P('fsdp', 'replica'), may hold values from -6 to 6
- prev_delta: bfloat16 [16, 3328, 3328], P('replica', 'fsdp'), may hold values from -4 to 4
- momentum: float32 [3328, 3328], P('fsdp', 'replica'), may hold values from -2 to 2
- pool: bfloat16 [16, 1024, 3328], P('replica', 'fsdp'), may hold values from -6 to 6
- ids: int32 [16, 2, 1024], P('replica', None, 'fsdp'), may hold values from 0 to 31
- cotangent: bfloat16 [16, 2, 3328, 1024], P('replica', None, 'fsdp'), may hold values from -6 to 6
Outputs:
- new_delta: bfloat16 [16, 3328, 3328], P('replica', 'fsdp')
- new_anchor: float32 [3328, 3328], P('fsdp', 'replica')
- new_momentum: float32 [3328, 3328], P('fsdp', 'replica')
All inputs are finite; a program needn't handle non-finite values.
Results may differ from a plain program's by a relative error of at most 0.0062.
Values may be sent and summed in bfloat16 or wider, within the bound.
No kernel may reach another device: no remote copies, remote signals or barrier semaphores. Data moves between devices by JAX's collectives and lax.ppermute only.
A program may use at most 64 MiB of HBM per device.

v0:
```python
import math

import jax
import jax.numpy as jnp
from jax import lax
from jax.sharding import PartitionSpec as P

D = 3328
HW = 3328


INNER_RATE = 2.0
INNER_DECAY = 0.1
PENALTY = 0.5
MOMENT_DECAY = 0.9
OUTER_RATE = 0.7
CLIP_SHARE = 0.05


def silu_slope(preact):
    sigmoid_val = jax.nn.sigmoid(preact)
    return sigmoid_val * (1.0 + preact * (1.0 - sigmoid_val))


def row_gradient(portion, rounded, cot_step, root_width):
    preact = (
        lax.dot_general(
            rounded, portion, (((1,), (1,)), ((), ())), preferred_element_type=jnp.float32
        )
        / root_width
    )
    scaled = (cot_step.astype(jnp.float32) * silu_slope(preact)).astype(jnp.bfloat16)
    return jnp.dot(scaled, portion, preferred_element_type=jnp.float32)


def island_mean(prev_delta):
    summed = lax.psum_scatter(
        prev_delta[0].astype(jnp.float32).astype(jnp.bfloat16),
        "replica",
        scatter_dimension=1,
        tiled=True,
    ).astype(jnp.float32)
    return summed / lax.axis_size("replica")


def body(anchor, prev_delta, momentum, pool, ids, cotangent):
    root_width = math.sqrt(D)
    anchor_island = lax.all_gather(anchor, "replica", axis=1, tiled=True)
    own_rows = jnp.take(pool[0], ids[0], axis=0)
    weights = anchor_island
    zero_grad = jnp.zeros(anchor_island.shape, jnp.float32)
    for inner_step in range(ids.shape[1]):
        rounded = weights.astype(jnp.bfloat16)
        cot_step = cotangent[0, inner_step]

        def accumulate(running, portion, first, rounded=rounded, cot_step=cot_step):
            return row_gradient(portion, rounded, cot_step, root_width)

        gradient = accumulate(
            zero_grad,
            lax.all_gather(own_rows[inner_step], "fsdp", axis=0, tiled=True),
            jnp.int32(0),
        )
        weights = weights - INNER_RATE * (gradient / root_width) - INNER_DECAY * weights
    new_delta = (anchor_island - weights).astype(jnp.bfloat16)[None]
    averaged = island_mean(prev_delta)
    corrected = averaged + PENALTY * (averaged - momentum)
    squares = lax.psum(jnp.sum(corrected * corrected), ("replica", "fsdp"))
    max_norm = CLIP_SHARE * math.sqrt(D * HW)
    factor = jnp.minimum(1.0, max_norm / jnp.sqrt(squares + 1e-06))
    clipped = factor * corrected
    new_momentum = MOMENT_DECAY * momentum + clipped
    new_anchor = anchor - OUTER_RATE * (MOMENT_DECAY * new_momentum + clipped)
    return (new_delta, new_anchor, new_momentum)


def solution(mesh):
    return jax.shard_map(
        body,
        mesh=mesh,
        in_specs=(
            P("fsdp", "replica"),
            P("replica", "fsdp", None),
            P("fsdp", "replica"),
            P("replica", "fsdp", None),
            P("replica", None, "fsdp"),
            P("replica", None, "fsdp", None),
        ),
        out_specs=(P("replica", "fsdp", None), P("fsdp", "replica"), P("fsdp", "replica")),
        check_vma=False,
    )
```

profile of v0, /device:TPU:1, one launch (start us, length us, event | category | flops | bytes accessed | tf_op | source)
XLA Modules:
  0.0 337.6 jit_solution(17442254707632525816)
XLA Ops:
  7.2 0.0 copy-start
  7.2 0.0 copy-start.3
  7.2 0.0 copy-start.4
  7.2 0.0 reduce-scatter.4.cloned.1.call-start
  7.2 2.4 copy.13
  9.6 0.0 reduce-scatter.4.cloned.1.call-update
  9.6 0.0 all-gather.6.cloned.1.call-start
  9.7 0.0 copy-done.3
  9.7 0.7 copy.9
  10.4 0.0 all-gather.6.cloned.1.call-update
  10.5 0.0 all-gather.8.cloned.1.call-start
  10.5 0.0 copy-done.4
  10.5 0.1 reshape.48
  10.6 0.0 copy-done
  10.6 0.8 gather_fusion
  11.5 0.0 copy-start.2
  11.5 0.1 broadcast_select_fusion
  11.6 0.8 fusion.76
  12.4 0.0 all-gather.8.cloned.1.call-update
  12.4 0.0 all-gather.10.cloned.1.call-start
  12.4 0.5 all-gather.10.cloned.1.call-update
  13.0 94.3 %reduce-scatter.4.cloned.1.call-done = bf16[208,104]{1,0:T(8,128)(2,1)} async-done(((bf16[3328,104]{1,0:T(8,128)(2,1)}), bf16[208,104]{1,0:T(8,128)(2,1)}) %reduce-scatter.4.cloned.1.call-update) | async-done | bytes 43280
  107.3 0.9 copy.14
  108.2 0.0 copy-done.2
  108.2 0.6 multiply_reduce_fusion
  108.9 99.5 %psum.7 = f32[]{:T(128)} all-reduce(f32[]{:T(128)} %multiply_reduce_fusion), channel_id=1, replica_groups=mesh['replica'=16,'fsdp'=32] {'replica','fsdp'}, use_global_device_ids=true, to_apply=%region_2.3 | all-reduce | flops 1 | bytes 8 | tf_op jit(solution)/shard_map/psum | solution.py:68
  209.1 0.7 multiply_subtract_fusion
  209.8 0.0 all-gather.6.cloned.1.call-done
  209.8 0.0 copy-start.1
  209.8 2.1 copy.12
  211.9 34.0 %all-gather.8.cloned.1.call-done = bf16[1,1024,3328]{2,1,0:T(8,128)(2,1)} async-done(((bf16[1,32,3328]{2,1,0:T(8,128)(2,1)}), bf16[1,1024,3328]{2,1,0:T(8,128)(2,1)}) %all-gather.8.cloned.1.call-update) | async-done | bytes 6815760 | tf_op jit(solution)/shard_map/all_gather | solution.py:61
  245.9 0.0 copy-done.1
  245.9 9.5 %fusion.26 = f32[104,3328]{1,0:T(8,128)} fusion(f32[104,3328]{1,0:T(8,128)S(1)} %copy.12, bf16[1,1024,3328]{2,1,0:T(8,128)(2,1)} %all-gather.8.cloned.1.call-done, f32[104,3328]{0,1:T(8,128)S(1)} %copy-done.1, bf16[1,2,104,1024]{3,2,1,0:T(8,128)(2,1)} %param.11), kind=kOutput, calls=%fused_computation.15 | convolution fusion | flops 1420576768 | bytes 17997824 | tf_op jit(solution)/shard_map/dot_general | solution.py:33
  255.4 65.7 %all-gather.10.cloned.1.call-done = bf16[1,1024,3328]{2,1,0:T(8,128)(2,1)} async-done(((bf16[1,32,3328]{2,1,0:T(8,128)(2,1)}), bf16[1,1024,3328]{2,1,0:T(8,128)(2,1)}) %all-gather.10.cloned.1.call-update) | async-done | bytes 6815760 | tf_op jit(solution)/shard_map/all_gather | solution.py:61
  321.1 10.0 %fusion.32 = bf16[1,104,3328]{2,1,0:T(8,128)(2,1)} fusion(f32[104,3328]{1,0:T(8,128)S(1)} %copy.12, f32[104,3328]{1,0:T(8,128)} %fusion.26, bf16[1,1024,3328]{2,1,0:T(8,128)(2,1)} %all-gather.10.cloned.1.call-done, bf16[1,2,104,1024]{3,2,1,0:T(8,128)(2,1)} %param.11), kind=kOutput, calls=%fused_computation.17 | convolution fusion | flops 1421268992 | bytes 18690048 | tf_op jit(solution)/shard_map/dot_general | solution.py:33
  (3 shorter events, 0.0 us)
Async XLA Ops:
  7.2 3.5 %copy-start = (bf16[1,32,3328]{2,1,0:T(8,128)(2,1)S(1)}, bf16[1,32,3328]{2,1,0:T(8,128)(2,1)}, u32[]{:S(2)}) copy-start(bf16[1,32,3328]{2,1,0:T(8,128)(2,1)} %param.9) | copy-start | bytes 638980
  7.2 2.5 copy-start.3
  7.2 3.3 copy-start.4
  7.2 100.1 %reduce-scatter.4.cloned.1.call-start = ((), (), s32[]{:S(2)}) async-start(), calls=%async_computation.4 | async-start | bytes 905216
  9.6 200.2 %all-gather.6.cloned.1.call-start = ((), (), s32[]{:S(2)}) async-start(), calls=%async_computation.1 | async-start | bytes 1810432 | tf_op jit(solution)/shard_map/all_gather | solution.py:48
  10.5 235.4 %all-gather.8.cloned.1.call-start = ((), (), s32[]{:S(2)}) async-start(), calls=%async_computation.2 | async-start | bytes 7028736 | tf_op jit(solution)/shard_map/all_gather | solution.py:61
  11.5 96.8 %copy-start.2 = (f32[104,208]{1,0:T(8,128)S(1)}, f32[104,208]{1,0:T(8,128)}, u32[]{:S(2)}) copy-start(f32[104,208]{1,0:T(8,128)} %param.8) | copy-start | bytes 259588
  12.4 308.7 %all-gather.10.cloned.1.call-start = ((), (), s32[]{:S(2)}) async-start(), calls=%async_computation.3 | async-start | bytes 7028736 | tf_op jit(solution)/shard_map/all_gather | solution.py:61
  209.8 36.1 %copy-start.1 = (f32[104,3328]{0,1:T(8,128)S(1)}, f32[104,3328]{0,1:T(8,128)}, u32[]{:S(2)}) copy-start(f32[104,3328]{0,1:T(8,128)} %all-gather.6.cloned.1.call-done) | copy-start | bytes 4153348
Sparse Core Ops, SparseCore 0:
  12.2 95.0 reduce-scatter.3
  110.4 60.5 all-gather.5
  173.1 72.7 all-gather.7
  248.5 72.6 all-gather.9
where the time goes:
time: 338 us
  waiting for transfers between devices  195 us (58%)
  blocking collectives  99.5 us (29%)
  matrix products  19.5 us (6%)
  between operations  14.6 us (4%)
  local copies, waits for them, and re-layouts  7.8 us (2%)
    all_gather x2, waiting for transfers between devices, body(): lax.all_gather(own_rows[inner_step], 'fsdp', axis=0, tiled=True)  99.7 us
    psum x1, blocking collectives, body(): squares = lax.psum(jnp.sum(corrected * corrected), ('replica', 'fsdp'))  99.5 us
    unnamed x5, waiting for transfers between devices  94.9 us
    dot_general x2, matrix products, row_gradient(): return jnp.dot(scaled, portion, preferred_element_type=jnp.float32)  19.5 us
  transfers between devices with their start and end apart: 4, of which 3 were waited for; matrix products, arithmetic and copies ran while one was open for 5% of the time, Pallas kernels for 0%

commit v1 on v0

v1 whole, which is shorter than its diff:
```python
import functools
import math

import jax
import jax.numpy as jnp
from jax import lax
from jax.experimental import pallas as pl
from jax.experimental.pallas import tpu as pltpu
from jax.sharding import Mesh
from jax.sharding import PartitionSpec as P

D = 3328
HW = 3328
TOK = 1024
ROWS = 104
BLOCK = 32
EXT = 128
CHUNK = 256
GROUP = 128
COLS = 256

INNER_RATE = 2.0
INNER_DECAY = 0.1
PENALTY = 0.5
MOMENT_DECAY = 0.9
OUTER_RATE = 0.7
CLIP_SHARE = 0.05

FSDP = ("zl", "y", "c")
REPLICA = ("x", "zh")


def silu_slope(preact):
    sigmoid_val = jax.nn.sigmoid(preact)
    return sigmoid_val * (1.0 + preact * (1.0 - sigmoid_val))


def inner_kernel(anchor_ref, cot_ref, pool_hbm, delta_ref, pool, weights, rounded, folded, sems):
    copies = []
    for zl in range(2):
        for half in range(2):
            rows = pl.ds(half * 8, 8)
            copy = pltpu.make_async_copy(
                pool_hbm.at[rows, zl], pool.at[zl, rows], sems.at[zl * 2 + half]
            )
            copy.start()
            copies.append(copy)
    root_width = math.sqrt(D)

    def picks(group, step):
        part = pool[group // 4, (group % 4) * 4 : (group % 4) * 4 + 4, :, D:]
        ids = part.reshape(GROUP, EXT)[:, step : step + 1].astype(jnp.float32).astype(jnp.int32)
        token = lax.broadcasted_iota(jnp.int32, (GROUP, GROUP), 0)
        row = lax.broadcasted_iota(jnp.int32, (GROUP, GROUP), 1)
        return jnp.where(row == (token // BLOCK) * BLOCK + ids, 1.0, 0.0).astype(jnp.bfloat16)

    for step in range(2):
        for chunk in range(TOK // CHUNK):
            if step == 0:
                copies[chunk].wait()
            left = anchor_ref[...] if step == 0 else rounded[...]
            block = pool[chunk // 2, (chunk % 2) * 8 : (chunk % 2) * 8 + 8, :, :D].reshape(CHUNK, D)
            all_rows = lax.dot_general(
                left, block, (((1,), (1,)), ((), ())), preferred_element_type=jnp.float32
            )
            for part in range(CHUNK // GROUP):
                group = chunk * (CHUNK // GROUP) + part
                picked = picks(group, step)
                tokens = slice(group * GROUP, (group + 1) * GROUP)
                values = all_rows[:, part * GROUP : (part + 1) * GROUP]
                preact = jnp.zeros((ROWS, GROUP), jnp.float32)
                for _ in range(3):
                    top = values.astype(jnp.bfloat16)
                    values = values - top.astype(jnp.float32)
                    preact = preact + lax.dot_general(
                        top, picked, (((1,), (1,)), ((), ())), preferred_element_type=jnp.float32
                    )
                preact = preact / root_width
                scaled = cot_ref[step, :, tokens].astype(jnp.float32) * silu_slope(preact)
                folded[:, tokens] = jnp.dot(
                    scaled.astype(jnp.bfloat16), picked, preferred_element_type=jnp.float32
                ).astype(jnp.bfloat16)
        for start in range(0, D, COLS):
            cols = slice(start, start + COLS)
            gradient = jnp.dot(
                folded[...],
                pool[:, :, :, cols].reshape(TOK, COLS),
                preferred_element_type=jnp.float32,
            )
            before = anchor_ref[:, cols].astype(jnp.float32)
            if step == 0:
                after = before - INNER_RATE * (gradient / root_width) - INNER_DECAY * before
                weights[:, cols] = after
                rounded[:, cols] = after.astype(jnp.bfloat16)
            else:
                last = weights[:, cols]
                after = last - INNER_RATE * (gradient / root_width) - INNER_DECAY * last
                delta_ref[:, cols] = (before - after).astype(jnp.bfloat16)


def inner_steps(anchor_island, cot, gathered):
    return pl.pallas_call(
        inner_kernel,
        out_shape=jax.ShapeDtypeStruct((ROWS, D), jnp.bfloat16),
        in_specs=[
            pl.BlockSpec(memory_space=pltpu.VMEM),
            pl.BlockSpec(memory_space=pltpu.VMEM),
            pl.BlockSpec(memory_space=pl.ANY),
        ],
        out_specs=pl.BlockSpec(memory_space=pltpu.VMEM),
        scratch_shapes=[
            pltpu.VMEM((2, 16, BLOCK, D + EXT), jnp.bfloat16),
            pltpu.VMEM((ROWS, D), jnp.float32),
            pltpu.VMEM((ROWS, D), jnp.bfloat16),
            pltpu.VMEM((ROWS, TOK), jnp.bfloat16),
            pltpu.SemaphoreType.DMA((4,)),
        ],
        compiler_params=pltpu.CompilerParams(vmem_limit_bytes=32 * 1024 * 1024),
        cost_estimate=pl.CostEstimate(
            flops=4 * 2 * ROWS * TOK * D, bytes_accessed=9_000_000, transcendentals=2 * ROWS * TOK
        ),
    )(anchor_island, cot, gathered)


def swap(value, axis, mask):
    count = lax.axis_size(axis)
    return lax.ppermute(value, axis, [(i, i ^ mask) for i in range(count)])


def doubled(value, axis, mask):
    other = swap(value, axis, mask)
    second = (lax.axis_index(axis) & mask) != 0
    return jnp.concatenate(
        [jnp.where(second, other, value), jnp.where(second, value, other)], axis=0
    )


def body(anchor, prev_delta, momentum, pool, ids, cotangent):
    sampled = jnp.pad(ids[0].T.astype(jnp.bfloat16), ((0, 0), (0, EXT - ids.shape[1])))
    rows = jnp.concatenate([pool[0], sampled], axis=1)[None]
    rows = doubled(rows, "zl", 1)
    gathered = lax.all_gather(rows, ("y", "c"), axis=0)

    sums = prev_delta[0].reshape(ROWS, 16, D // 16).transpose(1, 0, 2)
    sums = lax.all_to_all(sums, REPLICA, 0, 0)
    averaged = jnp.sum(sums.astype(jnp.float32), axis=0) / 16
    corrected = averaged + PENALTY * (averaged - momentum)
    squares = jnp.sum(corrected * corrected)
    for axes, count in ((FSDP, 32), (REPLICA, 16)):
        spread = jnp.broadcast_to(squares, (count, 8, 128))
        squares = jnp.sum(lax.all_to_all(spread, axes, 0, 0)[:, 0, 0])
    max_norm = CLIP_SHARE * math.sqrt(D * HW)
    factor = jnp.minimum(1.0, max_norm / jnp.sqrt(squares + 1e-06))
    clipped = factor * corrected
    new_momentum = MOMENT_DECAY * momentum + clipped
    new_anchor = anchor - OUTER_RATE * (MOMENT_DECAY * new_momentum + clipped)

    blocks = anchor.astype(jnp.bfloat16)[None]
    for axis, mask in (("zh", 1), ("zh", 2), ("x", 1), ("x", 2)):
        blocks = doubled(blocks, axis, mask)
    anchor_island = blocks.transpose(1, 0, 2).reshape(ROWS, D)
    new_delta = inner_steps(anchor_island, cotangent[0], gathered)[None]
    return (new_delta, new_anchor, new_momentum)


def solution(mesh):
    fine = Mesh(mesh.devices.reshape(4, 4, 2, 8, 2), REPLICA + FSDP)
    return jax.shard_map(
        body,
        mesh=fine,
        in_specs=(
            P(FSDP, REPLICA),
            P(REPLICA, FSDP, None),
            P(FSDP, REPLICA),
            P(REPLICA, FSDP, None),
            P(REPLICA, None, FSDP),
            P(REPLICA, None, FSDP, None),
        ),
        out_specs=(P(REPLICA, FSDP, None), P(FSDP, REPLICA), P(FSDP, REPLICA)),
        check_vma=False,
    )
```

time: 338 us -> 165 us (0.49)
  the two profiles are of different devices: /device:TPU:1 before, /device:TPU:8 now
where the time goes in v1:
time: 165 us; the launch traced here: 164 us
  blocking collectives  70.2 us (43%)
  waiting for transfers between devices  33.3 us (20%)
  Pallas kernels  15.6 us (9%)
  between operations  15 us (9%)
  starting transfers between devices  14.6 us (9%)
  local copies, waits for them, and re-layouts  9.14 us (6%)
  other arithmetic  6.73 us (4%)
    all_to_all x2, blocking collectives, body(): squares = jnp.sum(lax.all_to_all(spread, axes, 0, 0)[:, 0, 0])  36.2 us
    all_to_all x1, blocking collectives, body(): sums = lax.all_to_all(sums, REPLICA, 0, 0)  34 us
    ppermute x5, waiting for transfers between devices, swap(): return lax.ppermute(value, axis, [(i, i ^ mask) for i in range(count)])  33.3 us
    pallas_call x1, Pallas kernels, inner_steps(): pl.pallas_call(inner_kernel, out_shape=jax.ShapeDtypeStruct((ROWS, D), jn...  15.6 us
    ppermute x5, starting transfers between devices, swap(): return lax.ppermute(value, axis, [(i, i ^ mask) for i in range(count)])  14.6 us
  transfers between devices with their start and end apart: 6, of which 5 were waited for; matrix products, arithmetic and copies ran while one was open for 6% of the time, Pallas kernels for 0%

profile of v1, /device:TPU:8, one launch (start us, length us, event | category | flops | bytes accessed | tf_op | source)
XLA Modules:
  0.0 164.4 jit_solution(14399052070370696681)
XLA Ops:
  7.2 0.0 copy-start.2
  7.2 0.0 copy-start.3
  7.2 0.0 all-gather.3.cloned.1.call-start
  7.2 0.7 convert_bitcast_fusion.1
  7.9 0.1 copy.26
  8.1 1.0 fusion.2
  9.0 4.3 %collective-permute-start.4 = (bf16[1,32,3456]{2,1,0:T(8,128)(2,1)S(1)}, bf16[1,32,3456]{2,1,0:T(8,128)(2,1)S(1)}, u32[]{:S(2)}, u32[]{:S(2)}) collective-permute-start(bf16[1,32,3456]{2,1,0:T(8,128)(2,1)S(1)} %fusion.2), channel_id=1, source_target_pairs={{0,16},{16,0},{1,17},{17,1},{2,18},{18,2},{3,19},{19,3},{4,20},{20... | collective-permute-start | bytes 663560 | tf_op jit(solution)/shard_map/ppermute | solution.py:127
  13.3 5.4 %collective-permute-done.4 = bf16[1,32,3456]{2,1,0:T(8,128)(2,1)S(1)} collective-permute-done((bf16[1,32,3456]{2,1,0:T(8,128)(2,1)S(1)}, bf16[1,32,3456]{2,1,0:T(8,128)(2,1)S(1)}, u32[]{:S(2)}, u32[]{:S(2)}) %collective-permute-start.4) | collective-permute-done | bytes 221216 | tf_op jit(solution)/shard_map/ppermute | solution.py:127
  18.7 1.0 broadcast_select_fusion.3
  19.7 0.8 pad_maximum_fusion
  20.5 0.0 all-gather.3.cloned.1.call-update
  20.6 2.9 %reshape_squeeze.3 = bf16[104,16,208]{2,1,0:T(8,128)(2,1)S(1)} reshape(bf16[1,104,3328]{2,1,0:T(8,128)(2,1)} %param.7) | data formatting | bytes 1384448 | tf_op jit(solution)/shard_map/reshape;squeeze | solution.py:144
  23.4 0.3 copy.21
  23.7 0.0 copy-start.1
  23.7 34.0 %all_to_all.15 = bf16[16,104,208]{2,1,0:T(8,128)(2,1)S(1)} all-to-all(bf16[16,104,208]{2,1,0:T(8,128)(2,1)S(1)} %copy.21), channel_id=1, replica_groups=mesh['x'=4,'zh'=4,'zl'=2,'y'=8,'c'=2] {'x','zh'}, dimensions={0} | all-to-all | bytes 1384448 | tf_op jit(solution)/shard_map/all_to_all | solution.py:145
  57.7 0.1 convert_reduce_fusion
  57.8 0.0 copy-done.2
  57.8 0.6 multiply_reduce_fusion
  58.5 0.7 broadcast_in_dim.18
  59.1 21.5 %all_to_all.16 = f32[32,8,128]{2,1,0:T(8,128)S(1)} all-to-all(f32[32,8,128]{2,1,0:T(8,128)S(1)} %broadcast_in_dim.18), channel_id=1, replica_groups=mesh['x'=4,'zh'=4,'zl'=2,'y'=8,'c'=2] {'zl','y','c'}, dimensions={0} | all-to-all | bytes 262144 | tf_op jit(solution)/shard_map/all_to_all | solution.py:151
  80.6 0.6 slice_reduce_fusion
  81.3 0.6 broadcast_in_dim.19
  81.9 14.7 %all_to_all.17 = f32[16,8,128]{2,1,0:T(8,128)S(1)} all-to-all(f32[16,8,128]{2,1,0:T(8,128)S(1)} %broadcast_in_dim.19), channel_id=1, replica_groups=mesh['x'=4,'zh'=4,'zl'=2,'y'=8,'c'=2] {'x','zh'}, dimensions={0} | all-to-all | bytes 131072 | tf_op jit(solution)/shard_map/all_to_all | solution.py:151
  96.6 0.6 slice_reduce_fusion.1
  97.9 0.0 copy-done.3
  97.9 0.7 multiply_subtract_fusion
  98.7 2.5 %collective-permute-start = (bf16[1,104,208]{2,1,0:T(8,128)(2,1)S(1)}, bf16[1,104,208]{2,1,0:T(8,128)(2,1)S(1)}, u32[]{:S(2)}, u32[]{:S(2)}) collective-permute-start(bf16[1,104,208]{2,1,0:T(8,128)(2,1)S(1)} %get-tuple-element.13), channel_id=1, source_target_pairs={{0,32},{32,0},{64,96},{96,64},{1,33},{33,1},{65,97},{97,65},{2,34}... | collective-permute-start | bytes 129800 | tf_op jit(solution)/shard_map/ppermute | solution.py:127
  101.1 5.0 %collective-permute-done = bf16[1,104,208]{2,1,0:T(8,128)(2,1)S(1)} collective-permute-done((bf16[1,104,208]{2,1,0:T(8,128)(2,1)S(1)}, bf16[1,104,208]{2,1,0:T(8,128)(2,1)S(1)}, u32[]{:S(2)}, u32[]{:S(2)}) %collective-permute-start) | collective-permute-done | bytes 43296 | tf_op jit(solution)/shard_map/ppermute | solution.py:127
  106.2 2.6 %collective-permute-start.1 = (bf16[2,104,208]{2,1,0:T(8,128)(2,1)S(1)}, bf16[2,104,208]{2,1,0:T(8,128)(2,1)S(1)}, u32[]{:S(2)}, u32[]{:S(2)}) collective-permute-start(bf16[2,104,208]{2,1,0:T(8,128)(2,1)S(1)} %pad_maximum_fusion.3), channel_id=1, source_target_pairs={{0,64},{32,96},{64,0},{96,32},{1,65},{33,97},{65,1},{97,33},{2,66}... | collective-permute-start | bytes 259592 | tf_op jit(solution)/shard_map/ppermute | solution.py:127
  108.8 8.1 %collective-permute-done.1 = bf16[2,104,208]{2,1,0:T(8,128)(2,1)S(1)} collective-permute-done((bf16[2,104,208]{2,1,0:T(8,128)(2,1)S(1)}, bf16[2,104,208]{2,1,0:T(8,128)(2,1)S(1)}, u32[]{:S(2)}, u32[]{:S(2)}) %collective-permute-start.1) | collective-permute-done | bytes 86560 | tf_op jit(solution)/shard_map/ppermute | solution.py:127
  117.0 2.5 %collective-permute-start.2 = (bf16[4,104,208]{2,1,0:T(8,128)(2,1)S(1)}, bf16[4,104,208]{2,1,0:T(8,128)(2,1)S(1)}, u32[]{:S(2)}, u32[]{:S(2)}) collective-permute-start(bf16[4,104,208]{2,1,0:T(8,128)(2,1)S(1)} %pad_maximum_fusion.2), channel_id=1, source_target_pairs={{0,128},{128,0},{256,384},{384,256},{1,129},{129,1},{257,385},{385... | collective-permute-start | bytes 519176 | tf_op jit(solution)/shard_map/ppermute | solution.py:127
  119.5 5.9 %collective-permute-done.2 = bf16[4,104,208]{2,1,0:T(8,128)(2,1)S(1)} collective-permute-done((bf16[4,104,208]{2,1,0:T(8,128)(2,1)S(1)}, bf16[4,104,208]{2,1,0:T(8,128)(2,1)S(1)}, u32[]{:S(2)}, u32[]{:S(2)}) %collective-permute-start.2) | collective-permute-done | bytes 173088 | tf_op jit(solution)/shard_map/ppermute | solution.py:127
  125.4 0.1 broadcast_select_fusion.5
  125.5 0.1 pad_maximum_fusion.1
  125.6 2.7 %collective-permute-start.3 = (bf16[8,104,208]{2,1,0:T(8,128)(2,1)S(1)}, bf16[8,104,208]{2,1,0:T(8,128)(2,1)S(1)}, u32[]{:S(2)}, u32[]{:S(2)}) collective-permute-start(bf16[8,104,208]{2,1,0:T(8,128)(2,1)S(1)} %pad_maximum_fusion.1), channel_id=1, source_target_pairs={{0,256},{128,384},{256,0},{384,128},{1,257},{129,385},{257,1},{385... | collective-permute-start | bytes 1038344 | tf_op jit(solution)/shard_map/ppermute | solution.py:127
  128.3 8.8 %collective-permute-done.3 = bf16[8,104,208]{2,1,0:T(8,128)(2,1)S(1)} collective-permute-done((bf16[8,104,208]{2,1,0:T(8,128)(2,1)S(1)}, bf16[8,104,208]{2,1,0:T(8,128)(2,1)S(1)}, u32[]{:S(2)}, u32[]{:S(2)}) %collective-permute-start.3) | collective-permute-done | bytes 346144 | tf_op jit(solution)/shard_map/ppermute | solution.py:127
  137.1 0.1 broadcast_select_fusion.1
  137.2 0.1 maximum_bitcast_fusion
  137.4 0.2 copy.19
  137.5 1.4 reshape.10.anchor_ref
  139.0 0.0 all-gather.3.cloned.1.call-done
  139.0 0.0 copy-done.1
  139.0 0.0 copy-start
  139.0 3.0 %copy-done = bf16[32,32,3456]{2,1,0:T(8,128)(2,1)S(1)} copy-done((bf16[32,32,3456]{2,1,0:T(8,128)(2,1)S(1)}, bf16[32,32,3456]{2,1,0:T(8,128)(2,1)}, u32[]{:S(2)}) %copy-start) | copy-done | bytes 7077912
  142.0 15.6 %shard_map.85 = bf16[104,3328]{1,0:T(8,128)(2,1)} custom-call(bf16[104,3328]{1,0:T(8,128)(2,1)S(1)} %reshape.10.anchor_ref, bf16[2,104,1024]{2,1,0:T(8,128)(2,1)S(1)} %bitcast.20, bf16[16,2,32,3456]{3,2,1,0:T(8,128)(2,1)S(1)} %bitcast.19), custom_call_target="tpu_custom_call" | custom-call | flops 2835349504 | bytes 9000000 | tf_op jit(solution)/shard_map/pallas_call | solution.py:102
  (4 shorter events, 0.1 us)
Async XLA Ops:
  7.2 50.7 %copy-start.2 = (f32[104,208]{1,0:T(8,128)S(1)}, f32[104,208]{1,0:T(8,128)}, u32[]{:S(2)}) copy-start(f32[104,208]{1,0:T(8,128)} %param.8) | copy-start | bytes 259588
  7.2 90.7 %copy-start.3 = (f32[104,208]{1,0:T(8,128)S(1)}, f32[104,208]{1,0:T(8,128)}, u32[]{:S(2)}) copy-start(f32[104,208]{1,0:T(8,128)} %param.6) | copy-start | bytes 259588
  7.2 131.8 %all-gather.3.cloned.1.call-start = ((), (), s32[]{:S(2)}) async-start(), calls=%async_computation.3 | async-start | bytes 7520256 | tf_op jit(solution)/shard_map/all_gather | solution.py:142
  9.0 9.7 %collective-permute-start.4 = (bf16[1,32,3456]{2,1,0:T(8,128)(2,1)S(1)}, bf16[1,32,3456]{2,1,0:T(8,128)(2,1)S(1)}, u32[]{:S(2)}, u32[]{:S(2)}) collective-permute-start(bf16[1,32,3456]{2,1,0:T(8,128)(2,1)S(1)} %fusion.2), channel_id=1, source_target_pairs={{0,16},{16,0},{1,17},{17,1},{2,18},{18,2},{3,19},{19,3},{4,20},{20... | collective-permute-start | bytes 663560 | tf_op jit(solution)/shard_map/ppermute | solution.py:127
  23.7 115.3 %copy-start.1 = (bf16[1,2,104,1024]{3,2,1,0:T(8,128)(2,1)S(1)}, bf16[1,2,104,1024]{3,2,1,0:T(8,128)(2,1)}, u32[]{:S(2)}) copy-start(bf16[1,2,104,1024]{3,2,1,0:T(8,128)(2,1)} %param.11) | copy-start | bytes 1277956
  98.7 7.5 %collective-permute-start = (bf16[1,104,208]{2,1,0:T(8,128)(2,1)S(1)}, bf16[1,104,208]{2,1,0:T(8,128)(2,1)S(1)}, u32[]{:S(2)}, u32[]{:S(2)}) collective-permute-start(bf16[1,104,208]{2,1,0:T(8,128)(2,1)S(1)} %get-tuple-element.13), channel_id=1, source_target_pairs={{0,32},{32,0},{64,96},{96,64},{1,33},{33,1},{65,97},{97,65},{2,34}... | collective-permute-start | bytes 129800 | tf_op jit(solution)/shard_map/ppermute | solution.py:127
  106.2 10.8 %collective-permute-start.1 = (bf16[2,104,208]{2,1,0:T(8,128)(2,1)S(1)}, bf16[2,104,208]{2,1,0:T(8,128)(2,1)S(1)}, u32[]{:S(2)}, u32[]{:S(2)}) collective-permute-start(bf16[2,104,208]{2,1,0:T(8,128)(2,1)S(1)} %pad_maximum_fusion.3), channel_id=1, source_target_pairs={{0,64},{32,96},{64,0},{96,32},{1,65},{33,97},{65,1},{97,33},{2,66}... | collective-permute-start | bytes 259592 | tf_op jit(solution)/shard_map/ppermute | solution.py:127
  117.0 8.4 %collective-permute-start.2 = (bf16[4,104,208]{2,1,0:T(8,128)(2,1)S(1)}, bf16[4,104,208]{2,1,0:T(8,128)(2,1)S(1)}, u32[]{:S(2)}, u32[]{:S(2)}) collective-permute-start(bf16[4,104,208]{2,1,0:T(8,128)(2,1)S(1)} %pad_maximum_fusion.2), channel_id=1, source_target_pairs={{0,128},{128,0},{256,384},{384,256},{1,129},{129,1},{257,385},{385... | collective-permute-start | bytes 519176 | tf_op jit(solution)/shard_map/ppermute | solution.py:127
  125.6 11.5 %collective-permute-start.3 = (bf16[8,104,208]{2,1,0:T(8,128)(2,1)S(1)}, bf16[8,104,208]{2,1,0:T(8,128)(2,1)S(1)}, u32[]{:S(2)}, u32[]{:S(2)}) collective-permute-start(bf16[8,104,208]{2,1,0:T(8,128)(2,1)S(1)} %pad_maximum_fusion.1), channel_id=1, source_target_pairs={{0,256},{128,384},{256,0},{384,128},{1,257},{129,385},{257,1},{385... | collective-permute-start | bytes 1038344 | tf_op jit(solution)/shard_map/ppermute | solution.py:127
  139.0 3.0 %copy-start = (bf16[32,32,3456]{2,1,0:T(8,128)(2,1)S(1)}, bf16[32,32,3456]{2,1,0:T(8,128)(2,1)}, u32[]{:S(2)}) copy-start(bf16[32,32,3456]{2,1,0:T(8,128)(2,1)} %all-gather.3.cloned.1.call-done) | copy-start | bytes 21233668
Sparse Core Ops, SparseCore 0:
  20.7 56.3 all-gather.2

commit v2 on v1

--- a/solution.py
+++ b/solution.py
@@ -1,4 +1,3 @@
-import functools
 import math
 
 import jax
@@ -35,13 +34,15 @@
     return sigmoid_val * (1.0 + preact * (1.0 - sigmoid_val))
 
 
-def inner_kernel(anchor_ref, cot_ref, pool_hbm, delta_ref, pool, weights, rounded, folded, sems):
+def inner_kernel(
+    place_ref, anchor_ref, cot_ref, pool_hbm, delta_ref, pool, weights, rounded, folded, sems
+):
     copies = []
     for zl in range(2):
         for half in range(2):
             rows = pl.ds(half * 8, 8)
             copy = pltpu.make_async_copy(
-                pool_hbm.at[rows, zl], pool.at[zl, rows], sems.at[zl * 2 + half]
+                pool_hbm.at[rows, zl ^ place_ref[0]], pool.at[zl, rows], sems.at[zl * 2 + half]
             )
             copy.start()
             copies.append(copy)
@@ -98,16 +99,18 @@
                 delta_ref[:, cols] = (before - after).astype(jnp.bfloat16)
 
 
-def inner_steps(anchor_island, cot, gathered):
+def inner_steps(place, anchor_island, cot, gathered):
+    vmem = pl.BlockSpec(memory_space=pltpu.VMEM)
     return pl.pallas_call(
         inner_kernel,
         out_shape=jax.ShapeDtypeStruct((ROWS, D), jnp.bfloat16),
         in_specs=[
-            pl.BlockSpec(memory_space=pltpu.VMEM),
-            pl.BlockSpec(memory_space=pltpu.VMEM),
+            pl.BlockSpec(memory_space=pltpu.SMEM),
+            vmem,
+            vmem,
             pl.BlockSpec(memory_space=pl.ANY),
         ],
-        out_specs=pl.BlockSpec(memory_space=pltpu.VMEM),
+        out_specs=vmem,
         scratch_shapes=[
             pltpu.VMEM((2, 16, BLOCK, D + EXT), jnp.bfloat16),
             pltpu.VMEM((ROWS, D), jnp.float32),
@@ -115,11 +118,11 @@
             pltpu.VMEM((ROWS, TOK), jnp.bfloat16),
             pltpu.SemaphoreType.DMA((4,)),
         ],
-        compiler_params=pltpu.CompilerParams(vmem_limit_bytes=32 * 1024 * 1024),
+        compiler_params=pltpu.CompilerParams(vmem_limit_bytes=50 * 1024 * 1024),
         cost_estimate=pl.CostEstimate(
             flops=4 * 2 * ROWS * TOK * D, bytes_accessed=9_000_000, transcendentals=2 * ROWS * TOK
         ),
-    )(anchor_island, cot, gathered)
+    )(place, anchor_island, cot, gathered)
 
 
 def swap(value, axis, mask):
@@ -127,40 +130,54 @@
     return lax.ppermute(value, axis, [(i, i ^ mask) for i in range(count)])
 
 
-def doubled(value, axis, mask):
-    other = swap(value, axis, mask)
-    second = (lax.axis_index(axis) & mask) != 0
-    return jnp.concatenate(
-        [jnp.where(second, other, value), jnp.where(second, value, other)], axis=0
-    )
+def in_parts(value, shape):
+    lane = lax.broadcasted_iota(jnp.int32, shape, 1)
+    value = jnp.broadcast_to(value, shape)
+    top = value.astype(jnp.bfloat16)
+    rest = value - top.astype(jnp.float32)
+    middle = rest.astype(jnp.bfloat16)
+    last = (rest - middle.astype(jnp.float32)).astype(jnp.bfloat16)
+    return jnp.where(lane == 0, top, jnp.where(lane == 1, middle, last))
 
 
 def body(anchor, prev_delta, momentum, pool, ids, cotangent):
+    tie = lax.optimization_barrier
+    place = lax.axis_index("zl").reshape(1).astype(jnp.int32)
     sampled = jnp.pad(ids[0].T.astype(jnp.bfloat16), ((0, 0), (0, EXT - ids.shape[1])))
-    rows = jnp.concatenate([pool[0], sampled], axis=1)[None]
-    rows = doubled(rows, "zl", 1)
-    gathered = lax.all_gather(rows, ("y", "c"), axis=0)
+    rows = jnp.concatenate([pool[0], sampled], axis=1)
+    other_rows = swap(rows, "zl", 1)
+    sums = jnp.stack([prev_delta[0, :, i * (D // 4) : (i + 1) * (D // 4)] for i in range(4)])
+    sums = lax.all_to_all(sums, "x", 0, 0)
+    other_rows, sums = tie((other_rows, sums))
+    gathered = lax.all_gather(jnp.stack([rows, other_rows]), ("y", "c"), axis=0)
 
-    sums = prev_delta[0].reshape(ROWS, 16, D // 16).transpose(1, 0, 2)
-    sums = lax.all_to_all(sums, REPLICA, 0, 0)
-    averaged = jnp.sum(sums.astype(jnp.float32), axis=0) / 16
+    sums = jnp.sum(sums.astype(jnp.float32), axis=0)
+    width = D // 16
+    sums = jnp.stack([sums[:, i * width : (i + 1) * width] for i in range(4)])
+    blocks = jnp.broadcast_to(anchor.astype(jnp.bfloat16), (4, ROWS, width))
+    mixed = lax.all_to_all(
+        jnp.concatenate([sums.astype(jnp.bfloat16), blocks], axis=1), "zh", 0, 0
+    )
+    averaged = jnp.sum(mixed[:, :ROWS].astype(jnp.float32), axis=0) / 16
     corrected = averaged + PENALTY * (averaged - momentum)
-    squares = jnp.sum(corrected * corrected)
-    for axes, count in ((FSDP, 32), (REPLICA, 16)):
-        spread = jnp.broadcast_to(squares, (count, 8, 128))
-        squares = jnp.sum(lax.all_to_all(spread, axes, 0, 0)[:, 0, 0])
+    note = in_parts(jnp.sum(corrected * corrected, keepdims=True), (16, width))
+    blocks = jnp.concatenate([mixed[:, ROWS:].reshape(4 * ROWS, width), note], axis=0)
+    blocks = lax.all_to_all(jnp.broadcast_to(blocks, (4, *blocks.shape)), "x", 0, 0)
+    squares = jnp.sum(blocks[:, 4 * ROWS, :3].astype(jnp.float32))
+    anchor_island = (
+        blocks[:, : 4 * ROWS].reshape(16, ROWS, width).transpose(1, 0, 2).reshape(ROWS, D)
+    )
+    squares, anchor_island = tie((squares, anchor_island))
+    spread = lax.all_to_all(jnp.broadcast_to(squares, (128, 1, 128)), ("zh", *FSDP), 0, 0)
+    new_delta = inner_steps(place, anchor_island, cotangent[0], gathered)
+    spread, new_delta = tie((spread, new_delta))
+    squares = jnp.sum(spread[:, 0, 0])
     max_norm = CLIP_SHARE * math.sqrt(D * HW)
     factor = jnp.minimum(1.0, max_norm / jnp.sqrt(squares + 1e-06))
     clipped = factor * corrected
     new_momentum = MOMENT_DECAY * momentum + clipped
     new_anchor = anchor - OUTER_RATE * (MOMENT_DECAY * new_momentum + clipped)
-
-    blocks = anchor.astype(jnp.bfloat16)[None]
-    for axis, mask in (("zh", 1), ("zh", 2), ("x", 1), ("x", 2)):
-        blocks = doubled(blocks, axis, mask)
-    anchor_island = blocks.transpose(1, 0, 2).reshape(ROWS, D)
-    new_delta = inner_steps(anchor_island, cotangent[0], gathered)[None]
-    return (new_delta, new_anchor, new_momentum)
+    return (new_delta[None], new_anchor, new_momentum)
 
 
 def solution(mesh):

time: 165 us -> 114 us (0.69)
  the two profiles are of different devices: /device:TPU:8 before, /device:TPU:1 now
where the time goes in v2:
time: 114 us
  starting transfers between devices  43.3 us (38%)
  waiting for transfers between devices  21.3 us (19%)
  Pallas kernels  16.5 us (14%)
  between operations  16.2 us (14%)
  other arithmetic  8.33 us (7%)
  local copies, waits for them, and re-layouts  8.19 us (7%)
    all_to_all x1, starting transfers between devices, body(): lax.all_to_all(jnp.broadcast_to(squares, (128, 1, 128)), ('zh', *FSDP), 0...  19.4 us
    pallas_call x1, Pallas kernels, inner_steps(): pl.pallas_call(inner_kernel, out_shape=jax.ShapeDtypeStruct((ROWS, D), jn...  16.5 us
    all_to_all x1, starting transfers between devices, body(): lax.all_to_all(jnp.concatenate([sums.astype(jnp.bfloat16), blocks], axis=...  11.6 us
    all_to_all x1, waiting for transfers between devices, body(): lax.all_to_all(jnp.concatenate([sums.astype(jnp.bfloat16), blocks], axis=...  9.01 us
    all_to_all x1, waiting for transfers between devices, body(): lax.all_to_all(jnp.broadcast_to(blocks, (4, *blocks.shape)), 'x', 0, 0)  8.69 us
    all_to_all x1, starting transfers between devices, body(): sums = lax.all_to_all(sums, 'x', 0, 0)  4.84 us
    ppermute x1, starting transfers between devices, swap(): return lax.ppermute(value, axis, [(i, i ^ mask) for i in range(count)])  4 us
    ppermute x1, waiting for transfers between devices, swap(): return lax.ppermute(value, axis, [(i, i ^ mask) for i in range(count)])  3.6 us
  transfers between devices with their start and end apart: 6, of which 3 were waited for; matrix products, arithmetic and copies ran while one was open for 10% of the time, Pallas kernels for 14%

profile of v2, /device:TPU:1, one launch (start us, length us, event | category | flops | bytes accessed | tf_op | source)
XLA Modules:
  0.0 113.8 jit_solution(3888665553577373405)
XLA Ops:
  7.2 0.0 copy-start.2
  7.2 1.4 %fusion.3 = (bf16[1,104,832]{2,1,0:T(8,128)(2,1)S(1)}, bf16[1,104,832]{2,1,0:T(8,128)(2,1)S(1)}, bf16[1,104,832]{2,1,0:T(8,128)(2,1)S(1)}, bf16[1,104,832]{2,1,0:T(8,128)(2,1)S(1)}) fusion(bf16[1,104,3328]{2,1,0:T(8,128)(2,1)} %param.7), kind=kLoop, calls=%fused_computation.23 | loop fusion | bytes 1384448 | tf_op jit(solution)/shard_map/slice | solution.py:149
  8.6 1.0 pad_maximum_fusion
  9.6 4.8 %all-to-all-start = ((bf16[4,104,832]{2,1,0:T(8,128)(2,1)}), bf16[4,104,832]{2,1,0:T(8,128)(2,1)S(1)}, u32[]{:S(2)}, u32[]{:S(2)}) async-start(bf16[4,104,832]{2,1,0:T(8,128)(2,1)} %pad_maximum_fusion), calls=%async_computation | async-start | bytes 1490944 | tf_op jit(solution)/shard_map/all_to_all | solution.py:150
  14.4 0.0 all-gather.3.cloned.1.call-start
  14.5 0.7 convert_bitcast_fusion
  15.1 0.1 copy.34
  15.2 1.0 fusion.2
  16.2 4.0 %collective-permute-start = (bf16[32,3456]{1,0:T(8,128)(2,1)S(1)}, bf16[32,3456]{1,0:T(8,128)(2,1)S(1)}, u32[]{:S(2)}, u32[]{:S(2)}) collective-permute-start(bf16[32,3456]{1,0:T(8,128)(2,1)S(1)} %get-tuple-element.22), channel_id=1, source_target_pairs={{0,16},{16,0},{1,17},{17,1},{2,18},{18,2},{3,19},{19,3},{4,20},{20... | collective-permute-start | bytes 663560 | tf_op jit(solution)/shard_map/ppermute | solution.py:130
  20.2 3.6 %collective-permute-done = bf16[32,3456]{1,0:T(8,128)(2,1)S(1)} collective-permute-done((bf16[32,3456]{1,0:T(8,128)(2,1)S(1)}, bf16[32,3456]{1,0:T(8,128)(2,1)S(1)}, u32[]{:S(2)}, u32[]{:S(2)}) %collective-permute-start) | collective-permute-done | bytes 221216 | tf_op jit(solution)/shard_map/ppermute | solution.py:130
  23.8 0.0 all-to-all-done
  23.8 0.8 pad_maximum_fusion.1
  24.6 0.0 copy-start
  24.6 0.0 all-gather.3.cloned.1.call-update
  24.7 1.0 convert_element_type.49
  25.6 0.1 reduce.2
  25.7 0.1 slice_bitcast_fusion.3
  25.9 0.8 pad_maximum_fusion.2
  26.7 11.6 %all-to-all-start.1 = ((bf16[4,208,208]{2,1,0:T(8,128)(2,1)}), bf16[4,208,208]{2,1,0:T(8,128)(2,1)S(1)}, u32[]{:S(2)}, u32[]{:S(2)}) async-start(bf16[4,208,208]{2,1,0:T(8,128)(2,1)} %pad_maximum_fusion.2), calls=%async_computation.1 | async-start | bytes 851968 | tf_op jit(solution)/shard_map/all_to_all | solution.py:158
  38.3 9.0 %all-to-all-done.1 = bf16[4,208,208]{2,1,0:T(8,128)(2,1)S(1)} async-done(((bf16[4,208,208]{2,1,0:T(8,128)(2,1)}), bf16[4,208,208]{2,1,0:T(8,128)(2,1)S(1)}, u32[]{:S(2)}, u32[]{:S(2)}) %all-to-all-start.1) | async-done | bytes 346144 | tf_op jit(solution)/shard_map/all_to_all | solution.py:158
  47.4 0.0 copy-done.2
  47.4 0.6 multiply_reduce_fusion
  49.4 0.1 copy.28
  49.5 1.0 broadcast_in_dim.26
  50.5 3.5 %all-to-all-start.2 = ((bf16[4,432,208]{1,2,0:T(8,128)(2,1)}), bf16[4,432,208]{1,2,0:T(8,128)(2,1)S(1)}, u32[]{:S(2)}, u32[]{:S(2)}) async-start(bf16[4,432,208]{1,2,0:T(8,128)(2,1)} %broadcast_in_dim.26), calls=%async_computation.2 | async-start | bytes 1703936 | tf_op jit(solution)/shard_map/all_to_all | solution.py:165
  54.0 8.7 %all-to-all-done.2 = bf16[4,432,208]{1,2,0:T(8,128)(2,1)S(1)} async-done(((bf16[4,432,208]{1,2,0:T(8,128)(2,1)}), bf16[4,432,208]{1,2,0:T(8,128)(2,1)S(1)}, u32[]{:S(2)}, u32[]{:S(2)}) %all-to-all-start.2) | async-done | bytes 718880 | tf_op jit(solution)/shard_map/all_to_all | solution.py:165
  62.7 1.3 %copy.33 = bf16[4,416,208]{2,1,0:T(8,128)(2,1)} copy(bf16[4,416,208]{1,2,0:T(8,128)(2,1)S(1)} %bitcast.26) | data formatting | bytes 1384448
  64.0 0.0 copy-start.1
  64.0 1.4 %copy.30 = bf16[104,16,208]{2,1,0:T(8,128)(2,1)S(1)} copy(bf16[104,16,208]{2,0,1:T(8,128)(2,1)} %bitcast.27) | data formatting | bytes 1384448 | tf_op jit(solution)/shard_map/transpose | solution.py:168
  65.4 1.4 %reshape.23.anchor_ref = bf16[104,3328]{1,0:T(8,128)(2,1)S(1)} reshape(bf16[104,16,208]{2,1,0:T(8,128)(2,1)S(1)} %copy.30) | data formatting | bytes 1384448 | tf_op jit(solution)/shard_map/reshape | solution.py:168
  66.8 0.8 convert_reduce_fusion.1
  67.6 1.4 %broadcast_in_dim.27 = f32[128,1,128]{2,1,0:T(1,128)} broadcast(f32[]{:T(128)} %convert_reduce_fusion.1), dimensions={} | broadcast | bytes 65540 | tf_op jit(solution)/shard_map/broadcast_in_dim | solution.py:171
  68.9 19.4 %all-to-all-start.3 = ((f32[128,1,128]{2,1,0:T(1,128)}), f32[128,1,128]{2,1,0:T(1,128)S(1)}, u32[]{:S(2)}, u32[]{:S(2)}) async-start(f32[128,1,128]{2,1,0:T(1,128)} %broadcast_in_dim.27), calls=%async_computation.3 | async-start | bytes 131072 | tf_op jit(solution)/shard_map/all_to_all | solution.py:171
  88.3 0.0 all-gather.3.cloned.1.call-done
  88.3 0.0 copy-done
  88.3 16.5 %shard_map.85 = bf16[104,3328]{1,0:T(8,128)(2,1)} custom-call(s32[1]{0:T(128)} %bitcast.10.place_ref, bf16[104,3328]{1,0:T(8,128)(2,1)S(1)} %reshape.23.anchor_ref, bf16[2,104,1024]{2,1,0:T(8,128)(2,1)S(1)} %bitcast.25, bf16[16,2,32,3456]{3,2,1,0:T(8,128)(2,1)} %bitcast.31), custom_call_target="tpu_custom_call" | custom-call | flops 2835349504 | bytes 9000000 | tf_op jit(solution)/shard_map/pallas_call | solution.py:104
  104.8 0.0 all-to-all-done.3
  104.8 0.7 slice_reduce_fusion
  106.3 0.0 copy-done.1
  106.3 0.7 multiply_subtract_fusion
  (7 shorter events, 0.1 us)
Async XLA Ops:
  7.2 40.2 %copy-start.2 = (f32[104,208]{1,0:T(8,128)S(1)}, f32[104,208]{1,0:T(8,128)}, u32[]{:S(2)}) copy-start(f32[104,208]{1,0:T(8,128)} %param.8) | copy-start | bytes 259588
  9.6 14.2 %all-to-all-start = ((bf16[4,104,832]{2,1,0:T(8,128)(2,1)}), bf16[4,104,832]{2,1,0:T(8,128)(2,1)S(1)}, u32[]{:S(2)}, u32[]{:S(2)}) async-start(bf16[4,104,832]{2,1,0:T(8,128)(2,1)} %pad_maximum_fusion), calls=%async_computation | async-start | bytes 1490944 | tf_op jit(solution)/shard_map/all_to_all | solution.py:150
  14.4 73.9 %all-gather.3.cloned.1.call-start = ((), (), s32[]{:S(2)}) async-start(), calls=%async_computation.4 | async-start | bytes 7520256 | tf_op jit(solution)/shard_map/all_gather | solution.py:152
  16.2 7.6 %collective-permute-start = (bf16[32,3456]{1,0:T(8,128)(2,1)S(1)}, bf16[32,3456]{1,0:T(8,128)(2,1)S(1)}, u32[]{:S(2)}, u32[]{:S(2)}) collective-permute-start(bf16[32,3456]{1,0:T(8,128)(2,1)S(1)} %get-tuple-element.22), channel_id=1, source_target_pairs={{0,16},{16,0},{1,17},{17,1},{2,18},{18,2},{3,19},{19,3},{4,20},{20... | collective-permute-start | bytes 663560 | tf_op jit(solution)/shard_map/ppermute | solution.py:130
  24.6 63.7 %copy-start = (bf16[1,2,104,1024]{3,2,1,0:T(8,128)(2,1)S(1)}, bf16[1,2,104,1024]{3,2,1,0:T(8,128)(2,1)}, u32[]{:S(2)}) copy-start(bf16[1,2,104,1024]{3,2,1,0:T(8,128)(2,1)} %param.11) | copy-start | bytes 1277956
  26.7 20.6 %all-to-all-start.1 = ((bf16[4,208,208]{2,1,0:T(8,128)(2,1)}), bf16[4,208,208]{2,1,0:T(8,128)(2,1)S(1)}, u32[]{:S(2)}, u32[]{:S(2)}) async-start(bf16[4,208,208]{2,1,0:T(8,128)(2,1)} %pad_maximum_fusion.2), calls=%async_computation.1 | async-start | bytes 851968 | tf_op jit(solution)/shard_map/all_to_all | solution.py:158
  50.5 12.2 %all-to-all-start.2 = ((bf16[4,432,208]{1,2,0:T(8,128)(2,1)}), bf16[4,432,208]{1,2,0:T(8,128)(2,1)S(1)}, u32[]{:S(2)}, u32[]{:S(2)}) async-start(bf16[4,432,208]{1,2,0:T(8,128)(2,1)} %broadcast_in_dim.26), calls=%async_computation.2 | async-start | bytes 1703936 | tf_op jit(solution)/shard_map/all_to_all | solution.py:165
  64.0 42.3 %copy-start.1 = (f32[104,208]{1,0:T(8,128)S(1)}, f32[104,208]{1,0:T(8,128)}, u32[]{:S(2)}) copy-start(f32[104,208]{1,0:T(8,128)} %param.6) | copy-start | bytes 259588
  68.9 35.9 %all-to-all-start.3 = ((f32[128,1,128]{2,1,0:T(1,128)}), f32[128,1,128]{2,1,0:T(1,128)S(1)}, u32[]{:S(2)}, u32[]{:S(2)}) async-start(f32[128,1,128]{2,1,0:T(1,128)} %broadcast_in_dim.27), calls=%async_computation.3 | async-start | bytes 131072 | tf_op jit(solution)/shard_map/all_to_all | solution.py:171
Sparse Core Ops, SparseCore 0:
  24.8 58.7 all-gather.2

commit v3 on v2

v3 whole, which is shorter than its diff:
```python
import math

import jax
import jax.numpy as jnp
from jax import lax
from jax.experimental import pallas as pl
from jax.experimental.pallas import tpu as pltpu
from jax.sharding import Mesh
from jax.sharding import PartitionSpec as P

D = 3328
HW = 3328
TOK = 1024
ROWS = 104
BLOCK = 32
EXT = 128
CHUNK = 256
COLS = 256
WIDTH = D // 16

INNER_RATE = 2.0
INNER_DECAY = 0.1
PENALTY = 0.5
MOMENT_DECAY = 0.9
OUTER_RATE = 0.7
CLIP_SHARE = 0.05

FSDP = ("zl", "y", "c")
REPLICA = ("x", "zh")


def silu_slope(preact):
    sigmoid_val = jax.nn.sigmoid(preact)
    return sigmoid_val * (1.0 + preact * (1.0 - sigmoid_val))


def inner_kernel(
    place_ref, anchor_ref, cot_ref, pool_hbm, delta_ref, pool, weights, rounded, folded, sems
):
    copies = []
    for zl in range(2):
        for half in range(2):
            rows = pl.ds(half * 8, 8)
            copy = pltpu.make_async_copy(
                pool_hbm.at[rows, zl ^ place_ref[0]], pool.at[zl, rows], sems.at[zl * 2 + half]
            )
            copy.start()
            copies.append(copy)
    root_width = math.sqrt(D)

    def picks(chunk, step):
        part = pool[chunk // 2, (chunk % 2) * 8 : (chunk % 2) * 8 + 8, :, D:]
        ids = part.reshape(CHUNK, EXT)[:, step : step + 1].astype(jnp.float32).astype(jnp.int32)
        token = lax.broadcasted_iota(jnp.int32, (CHUNK, CHUNK), 0)
        row = lax.broadcasted_iota(jnp.int32, (CHUNK, CHUNK), 1)
        return jnp.where(row == (token // BLOCK) * BLOCK + ids, 1.0, 0.0).astype(jnp.bfloat16)

    def project(chunk, step):
        if step == 0:
            copies[chunk].wait()
        left = anchor_ref[...] if step == 0 else rounded[...]
        block = pool[chunk // 2, (chunk % 2) * 8 : (chunk % 2) * 8 + 8, :, :D].reshape(CHUNK, D)
        return lax.dot_general(
            left, block, (((1,), (1,)), ((), ())), preferred_element_type=jnp.float32
        )

    def fold(chunk, step, values):
        picked = picks(chunk, step)
        tokens = slice(chunk * CHUNK, (chunk + 1) * CHUNK)
        preact = jnp.zeros((ROWS, CHUNK), jnp.float32)
        for _ in range(3):
            top = values.astype(jnp.bfloat16)
            values = values - top.astype(jnp.float32)
            preact = preact + lax.dot_general(
                top, picked, (((1,), (1,)), ((), ())), preferred_element_type=jnp.float32
            )
        preact = preact / root_width
        scaled = cot_ref[step, :, tokens].astype(jnp.float32) * silu_slope(preact)
        folded[:, tokens] = jnp.dot(
            scaled.astype(jnp.bfloat16), picked, preferred_element_type=jnp.float32
        ).astype(jnp.bfloat16)

    for step in range(2):
        values = project(0, step)
        for chunk in range(1, TOK // CHUNK):
            later = project(chunk, step)
            fold(chunk - 1, step, values)
            values = later
        fold(TOK // CHUNK - 1, step, values)
        for start in range(0, D, COLS):
            cols = slice(start, start + COLS)
            gradient = jnp.dot(
                folded[...],
                pool[:, :, :, cols].reshape(TOK, COLS),
                preferred_element_type=jnp.float32,
            )
            before = anchor_ref[:, cols].astype(jnp.float32)
            if step == 0:
                after = before - INNER_RATE * (gradient / root_width) - INNER_DECAY * before
                weights[:, cols] = after
                rounded[:, cols] = after.astype(jnp.bfloat16)
            else:
                last = weights[:, cols]
                after = last - INNER_RATE * (gradient / root_width) - INNER_DECAY * last
                delta_ref[:, cols] = (before - after).astype(jnp.bfloat16)


def inner_steps(place, anchor_island, cot, gathered):
    vmem = pl.BlockSpec(memory_space=pltpu.VMEM)
    return pl.pallas_call(
        inner_kernel,
        out_shape=jax.ShapeDtypeStruct((ROWS, D), jnp.bfloat16),
        in_specs=[
            pl.BlockSpec(memory_space=pltpu.SMEM),
            vmem,
            vmem,
            pl.BlockSpec(memory_space=pl.ANY),
        ],
        out_specs=vmem,
        scratch_shapes=[
            pltpu.VMEM((2, 16, BLOCK, D + EXT), jnp.bfloat16),
            pltpu.VMEM((ROWS, D), jnp.float32),
            pltpu.VMEM((ROWS, D), jnp.bfloat16),
            pltpu.VMEM((ROWS, TOK), jnp.bfloat16),
            pltpu.SemaphoreType.DMA((4,)),
        ],
        compiler_params=pltpu.CompilerParams(vmem_limit_bytes=50 * 1024 * 1024),
        cost_estimate=pl.CostEstimate(
            flops=4 * 2 * ROWS * TOK * D, bytes_accessed=9_000_000, transcendentals=2 * ROWS * TOK
        ),
    )(place, anchor_island, cot, gathered)


def swap(value, axis, mask):
    count = lax.axis_size(axis)
    return lax.ppermute(value, axis, [(i, i ^ mask) for i in range(count)])


def small_call(kernel, out_shapes, *args, limit=8):
    vmem = pl.BlockSpec(memory_space=pltpu.VMEM)
    return pl.pallas_call(
        kernel,
        out_shape=[jax.ShapeDtypeStruct(shape, dtype) for shape, dtype in out_shapes],
        in_specs=[vmem] * len(args),
        out_specs=[vmem] * len(out_shapes),
        compiler_params=pltpu.CompilerParams(vmem_limit_bytes=limit * 1024 * 1024),
    )(*args)


def pack_kernel(
    delta_ref, pool_ref, ids_ref, anchor_ref, momentum_ref, sums_ref, rows_ref, rounded_ref, held_ref
):
    rounded_ref[...] = anchor_ref[...].astype(jnp.bfloat16)
    held_ref[...] = momentum_ref[...]
    part = D // 4
    for i in range(4):
        sums_ref[i] = delta_ref[0, :, i * part : (i + 1) * part]
    rows_ref[:, :D] = pool_ref[0]
    ids = ids_ref[0].astype(jnp.float32)
    square = (BLOCK, BLOCK)
    diagonal = lax.broadcasted_iota(jnp.int32, square, 0) == lax.broadcasted_iota(jnp.int32, square, 1)
    lane = lax.broadcasted_iota(jnp.int32, (BLOCK, EXT), 1)
    extra = jnp.zeros((BLOCK, EXT), jnp.float32)
    for step in range(2):
        row = jnp.broadcast_to(ids[step : step + 1], square)
        column = jnp.sum(jnp.where(diagonal, row, 0.0), axis=1, keepdims=True)
        extra = jnp.where(lane == step, jnp.broadcast_to(column, extra.shape), extra)
    rows_ref[:, D:] = extra.astype(jnp.bfloat16)


def middle_kernel(sums_ref, anchor_ref, out_ref):
    sums = sum(sums_ref[i].astype(jnp.float32) for i in range(4))
    for i in range(4):
        out_ref[i, 0] = sums[:, i * WIDTH : (i + 1) * WIDTH].astype(jnp.bfloat16)
        out_ref[i, 1] = anchor_ref[...]


def square_kernel(mixed_ref, momentum_ref, corrected_ref, out_ref):
    averaged = sum(mixed_ref[i, 0].astype(jnp.float32) for i in range(4)) / 16
    corrected = averaged + PENALTY * (averaged - momentum_ref[...])
    corrected_ref[...] = corrected
    squares = jnp.sum(corrected * corrected, axis=(0, 1), keepdims=True)
    shape = (ROWS, 256 - WIDTH)
    lane = lax.broadcasted_iota(jnp.int32, shape, 1)
    squares = jnp.broadcast_to(squares, shape)
    top = squares.astype(jnp.bfloat16).astype(jnp.float32)
    middle = (squares - top).astype(jnp.bfloat16).astype(jnp.float32)
    note = jnp.where(lane == 0, top, jnp.where(lane == 1, middle, squares - top - middle))
    note = jnp.where(lane < 3, note, 0.0).astype(jnp.bfloat16)
    for i in range(4):
        for j in range(4):
            out_ref[i, j, :, :WIDTH] = mixed_ref[j, 1]
            out_ref[i, j, :, WIDTH:] = note


def unpack_kernel(blocks_ref, anchor_ref, spread_ref):
    shape = (ROWS, 128)
    lane = lax.broadcasted_iota(jnp.int32, shape, 1)
    row = lax.broadcasted_iota(jnp.int32, shape, 0)
    squares = jnp.zeros(shape, jnp.float32)
    for i in range(4):
        for j in range(4):
            place = (i * 4 + j) * WIDTH
            anchor_ref[:, place : place + WIDTH] = blocks_ref[i, j, :, :WIDTH]
        squares = squares + blocks_ref[i, 0, :, 128:].astype(jnp.float32)
    squares = jnp.where((row == 0) & (lane >= WIDTH - 128), squares, 0.0)
    squares = jnp.sum(squares, axis=(0, 1), keepdims=True)
    spread_ref[...] = jnp.broadcast_to(squares.reshape(1, 1, 1), spread_ref.shape)


def outer_kernel(spread_ref, corrected_ref, momentum_ref, anchor_ref, new_anchor_ref, new_momentum_ref):
    squares = jnp.sum(spread_ref[...], axis=0)[:, :1]
    max_norm = CLIP_SHARE * math.sqrt(D * HW)
    factor = jnp.minimum(1.0, max_norm / jnp.sqrt(squares + 1e-06))
    clipped = factor * corrected_ref[...]
    new_momentum = MOMENT_DECAY * momentum_ref[...] + clipped
    new_momentum_ref[...] = new_momentum
    new_anchor_ref[...] = anchor_ref[...] - OUTER_RATE * (MOMENT_DECAY * new_momentum + clipped)


def body(anchor, prev_delta, momentum, pool, ids, cotangent):
    tie = lax.optimization_barrier
    bf16, f32 = jnp.bfloat16, jnp.float32
    block = (ROWS, WIDTH)
    place = lax.axis_index("zl").reshape(1).astype(jnp.int32)
    sums, rows, rounded, held = small_call(
        pack_kernel,
        [((4, ROWS, D // 4), bf16), ((BLOCK, D + EXT), bf16), (block, bf16), (block, f32)],
        prev_delta,
        pool,
        ids,
        anchor,
        momentum,
        limit=56,
    )
    sums = lax.all_to_all(sums, "x", 0, 0)
    other_rows, sums = tie((swap(rows, "zl", 1), sums))
    gathered = lax.all_gather(jnp.stack([rows, other_rows]), ("y", "c"), axis=0)

    (mixed,) = small_call(middle_kernel, [((4, 2, *block), bf16)], sums, rounded)
    mixed = lax.all_to_all(mixed, "zh", 0, 0)
    corrected, blocks = small_call(
        square_kernel, [(block, f32), ((4, 4, ROWS, 256), bf16)], mixed, held
    )
    blocks = lax.all_to_all(blocks, "x", 0, 0)
    anchor_island, spread = small_call(
        unpack_kernel, [((ROWS, D), bf16), ((128, 1, 128), f32)], blocks
    )
    spread = lax.all_to_all(spread, ("zh", *FSDP), 0, 0)
    new_delta = inner_steps(place, anchor_island, cotangent[0], gathered)
    spread, new_delta = tie((spread, new_delta))
    new_anchor, new_momentum = small_call(
        outer_kernel, [(block, f32), (block, f32)], spread, corrected, momentum, anchor
    )
    return (new_delta[None], new_anchor, new_momentum)


def solution(mesh):
    fine = Mesh(mesh.devices.reshape(4, 4, 2, 8, 2), REPLICA + FSDP)
    return jax.shard_map(
        body,
        mesh=fine,
        in_specs=(
            P(FSDP, REPLICA),
            P(REPLICA, FSDP, None),
            P(FSDP, REPLICA),
            P(REPLICA, FSDP, None),
            P(REPLICA, None, FSDP),
            P(REPLICA, None, FSDP, None),
        ),
        out_specs=(P(REPLICA, FSDP, None), P(FSDP, REPLICA), P(FSDP, REPLICA)),
        check_vma=False,
    )
```

time: 114 us -> 104 us (0.912)
  blocking collectives: 0 us -> 22.5 us
  starting transfers between devices: 43.3 us -> 31.4 us
  waiting for transfers between devices: 21.3 us -> 14.4 us
  other arithmetic: 8.33 us -> 1.75 us
  local copies, waits for them, and re-layouts: 8.19 us -> 1.75 us
  between operations: 16.2 us -> 14.1 us
  Pallas kernels: 16.5 us -> 17.7 us
    all_to_all x0 -> x1, blocking collectives: none -> 22.5 us  [body(): mixed = lax.all_to_all(mixed, 'zh', 0, 0)]
    all_to_all x3 -> x2, starting transfers between devices: 34.5 us -> 22.6 us  [the longest x1 19.1 us: body(): spread = lax.all_to_all(spread, ('zh', *FSDP), 0, 0)]
    all_to_all x3 -> x2, waiting for transfers between devices: 17.7 us -> 8.7 us  [the longest x1 8.69 us: body(): blocks = lax.all_to_all(blocks, 'x', 0, 0)]
    pallas_call x0 -> x5, Pallas kernels: none -> 5.74 us  [small_call(): pl.pallas_call(kernel, out_shape=[jax.ShapeDtypeStruct(shape, dtype) for...]
    pallas_call x1, Pallas kernels: 16.5 us -> 12 us  [inner_steps(): pl.pallas_call(inner_kernel, out_shape=jax.ShapeDtypeStruct((ROWS, D), jn...]
    broadcast_in_dim x3 -> x0, local copies, waits for them, and re-layouts: 2.34 us -> none  [the longest x1 1.35 us: body(): jnp.broadcast_to(squares, (128, 1, 128))]
    reduce_sum x5 -> x0, other arithmetic: 2.28 us -> none  [the longest x1 0.76 us: body(): squares = jnp.sum(blocks[:, 4 * ROWS, :3].astype(jnp.float32))]
    convert_element_type x2 -> x0, other arithmetic: 1.63 us -> none  [the longest x1 0.95 us: body(): blocks = jnp.broadcast_to(anchor.astype(jnp.bfloat16), (4, ROWS, width))]
  transfers between devices with their start and end apart: 6 -> 5, of which waited for: 3 -> 4; matrix products, arithmetic and copies ran while one was open for 10% -> 0% of each run, Pallas kernels for 14% -> 14%
where the time goes in v3:
time: 104 us
  starting transfers between devices  31.4 us (30%)
  blocking collectives  22.5 us (22%)
  Pallas kernels  17.7 us (17%)
  waiting for transfers between devices  14.4 us (14%)
  between operations  14.1 us (14%)
  local copies, waits for them, and re-layouts  1.75 us (2%)
  other arithmetic  1.75 us (2%)
    all_to_all x1, blocking collectives, body(): mixed = lax.all_to_all(mixed, 'zh', 0, 0)  22.5 us
    all_to_all x1, starting transfers between devices, body(): spread = lax.all_to_all(spread, ('zh', *FSDP), 0, 0)  19.1 us
    pallas_call x1, Pallas kernels, inner_steps(): pl.pallas_call(inner_kernel, out_shape=jax.ShapeDtypeStruct((ROWS, D), jn...  12 us
    all_to_all x1, waiting for transfers between devices, body(): blocks = lax.all_to_all(blocks, 'x', 0, 0)  8.69 us
    pallas_call x5, Pallas kernels, small_call(): pl.pallas_call(kernel, out_shape=[jax.ShapeDtypeStruct(shape, dtype) for...  5.74 us
    all_to_all x1, starting transfers between devices, body(): sums = lax.all_to_all(sums, 'x', 0, 0)  4.84 us
    ppermute x1, starting transfers between devices, swap(): return lax.ppermute(value, axis, [(i, i ^ mask) for i in range(count)])  3.99 us
    ppermute x1, waiting for transfers between devices, swap(): return lax.ppermute(value, axis, [(i, i ^ mask) for i in range(count)])  3.52 us
  transfers between devices with their start and end apart: 5, of which 4 were waited for; matrix products, arithmetic and copies ran while one was open for 0% of the time, Pallas kernels for 14%

profile of v3, /device:TPU:1, one launch (start us, length us, event | category | flops | bytes accessed | tf_op | source)
XLA Modules:
  0.0 103.7 jit_solution(7778119288507758948)
XLA Ops:
  7.2 0.0 copy-start.4
  7.2 2.5 %shard_map.85 = (bf16[4,104,832]{2,1,0:T(8,128)(2,1)}, bf16[32,3456]{1,0:T(8,128)(2,1)}, bf16[104,208]{1,0:T(8,128)(2,1)}, f32[104,208]{1,0:T(8,128)}) custom-call(bf16[1,104,3328]{2,1,0:T(8,128)(2,1)} %delta_ref.1, bf16[1,32,3328]{2,1,0:T(8,128)(2,1)} %pool_ref.1, s32[1,2,32]{2,1,0:T(2,128)} %ids_ref.1, f32[104,208]{1,0:T(8,128)} %anchor_ref.3, ...), custom_call_target="tpu_custom_call" | custom-call | tf_op jit(solution)/shard_map/pallas_call | solution.py:141
  9.7 4.8 %all-to-all-start = ((bf16[4,104,832]{2,1,0:T(8,128)(2,1)}), bf16[4,104,832]{2,1,0:T(8,128)(2,1)S(1)}, u32[]{:S(2)}, u32[]{:S(2)}) async-start(bf16[4,104,832]{2,1,0:T(8,128)(2,1)} %get-tuple-element.18), calls=%async_computation | async-start | bytes 1490944 | tf_op jit(solution)/shard_map/all_to_all | solution.py:236
  14.6 0.0 all-gather.3.cloned.1.call-start
  14.6 4.0 %collective-permute-start = (bf16[32,3456]{1,0:T(8,128)(2,1)}, bf16[32,3456]{1,0:T(8,128)(2,1)S(1)}, u32[]{:S(2)}, u32[]{:S(2)}) collective-permute-start(bf16[32,3456]{1,0:T(8,128)(2,1)} %get-tuple-element.17), channel_id=1, source_target_pairs={{0,16},{16,0},{1,17},{17,1},{2,18},{18,2},{3,19},{19,3},{4,20},{20... | collective-permute-start | bytes 663560 | tf_op jit(solution)/shard_map/ppermute | solution.py:136
  18.6 3.5 %collective-permute-done = bf16[32,3456]{1,0:T(8,128)(2,1)S(1)} collective-permute-done((bf16[32,3456]{1,0:T(8,128)(2,1)}, bf16[32,3456]{1,0:T(8,128)(2,1)S(1)}, u32[]{:S(2)}, u32[]{:S(2)}) %collective-permute-start) | collective-permute-done | bytes 221216 | tf_op jit(solution)/shard_map/ppermute | solution.py:136
  22.1 0.6 all-to-all-done.sums_ref
  22.7 1.7 %pad_maximum_fusion = bf16[2,32,3456]{2,1,0:T(8,128)(2,1)} fusion(bf16[1,32,3456]{2,1,0:T(8,128)(2,1)S(1)} %bitcast.8, bf16[1,32,3456]{2,1,0:T(8,128)(2,1)} %bitcast.7), kind=kLoop, calls=%fused_computation | loop fusion | flops 221184 | bytes 884736 | tf_op jit(solution)/shard_map/stack | solution.py:238
  24.4 0.0 all-gather.3.cloned.1.call-update
  24.4 0.0 copy-start.3
  24.5 0.8 copy-done.3
  25.3 0.2 shard_map.86
  25.4 22.5 %all_to_all.20.mixed_ref = bf16[4,2,104,208]{3,2,1,0:T(8,128)(2,1)S(1)} all-to-all(bf16[4,2,104,208]{3,2,1,0:T(8,128)(2,1)S(1)} %shard_map.86), channel_id=1, replica_groups=mesh['x'=4,'zh'=4,'zl'=2,'y'=8,'c'=2] {'zh'}, dimensions={0} | all-to-all | bytes 692224 | tf_op jit(solution)/shard_map/all_to_all | solution.py:241
  47.9 0.0 copy-start
  47.9 0.0 copy-start.1
  47.9 0.0 copy-start.2
  47.9 0.9 copy-done.2
  48.9 1.2 %shard_map.87 = (f32[104,208]{1,0:T(8,128)S(1)}, bf16[4,4,104,256]{3,2,1,0:T(8,128)(2,1)}) custom-call(bf16[4,2,104,208]{3,2,1,0:T(8,128)(2,1)S(1)} %all_to_all.20.mixed_ref, f32[104,208]{1,0:T(8,128)S(1)} %copy-done.2), custom_call_target="tpu_custom_call" | custom-call | tf_op jit(solution)/shard_map/pallas_call | solution.py:141
  50.1 3.5 %all-to-all-start.2 = ((bf16[4,4,104,256]{3,2,1,0:T(8,128)(2,1)}), bf16[4,4,104,256]{3,2,1,0:T(8,128)(2,1)S(1)}, u32[]{:S(2)}, u32[]{:S(2)}) async-start(bf16[4,4,104,256]{3,2,1,0:T(8,128)(2,1)} %get-tuple-element.22), calls=%async_computation.2 | async-start | bytes 1703936 | tf_op jit(solution)/shard_map/all_to_all | solution.py:245
  53.6 8.7 %all-to-all-done.2.blocks_ref = bf16[4,4,104,256]{3,2,1,0:T(8,128)(2,1)S(1)} async-done(((bf16[4,4,104,256]{3,2,1,0:T(8,128)(2,1)}), bf16[4,4,104,256]{3,2,1,0:T(8,128)(2,1)S(1)}, u32[]{:S(2)}, u32[]{:S(2)}) %all-to-all-start.2) | async-done | bytes 852000 | tf_op jit(solution)/shard_map/all_to_all | solution.py:245
  62.3 0.9 shard_map.88
  63.2 19.1 %all-to-all-start.3 = ((f32[128,1,128]{2,1,0:T(1,128)}), f32[128,1,128]{2,1,0:T(1,128)S(1)}, u32[]{:S(2)}, u32[]{:S(2)}) async-start(f32[128,1,128]{2,1,0:T(1,128)} %get-tuple-element.23), calls=%async_computation.3 | async-start | bytes 131072 | tf_op jit(solution)/shard_map/all_to_all | solution.py:249
  82.3 1.6 %all-gather.3.cloned.1.call-done = bf16[32,32,3456]{2,1,0:T(8,128)(2,1)} async-done(((bf16[2,32,3456]{2,1,0:T(8,128)(2,1)}), bf16[32,32,3456]{2,1,0:T(8,128)(2,1)}) %all-gather.3.cloned.1.call-update) | async-done | bytes 7077904 | tf_op jit(solution)/shard_map/all_gather | solution.py:238
  83.9 0.0 copy-done.4
  83.9 12.0 %shard_map.89 = bf16[104,3328]{1,0:T(8,128)(2,1)} custom-call(s32[1]{0:T(128)} %bitcast.place_ref, bf16[104,3328]{1,0:T(8,128)(2,1)S(1)} %get-tuple-element.24.anchor_ref, bf16[2,104,1024]{2,1,0:T(8,128)(2,1)S(1)} %bitcast.6, bf16[16,2,32,3456]{3,2,1,0:T(8,128)(2,1)} %bitcast.9), custom_call_target="tpu_custom_call" | custom-call | flops 2835349504 | bytes 9000000 | tf_op jit(solution)/shard_map/pallas_call | solution.py:110
  95.9 0.0 all-to-all-done.3.spread_ref
  95.9 0.0 copy-done
  95.9 0.0 copy-done.1
  95.9 0.9 shard_map.90
Async XLA Ops:
  7.2 76.7 %copy-start.4 = (bf16[1,2,104,1024]{3,2,1,0:T(8,128)(2,1)S(1)}, bf16[1,2,104,1024]{3,2,1,0:T(8,128)(2,1)}, u32[]{:S(2)}) copy-start(bf16[1,2,104,1024]{3,2,1,0:T(8,128)(2,1)} %param.11) | copy-start | bytes 1277956
  9.7 13.0 %all-to-all-start = ((bf16[4,104,832]{2,1,0:T(8,128)(2,1)}), bf16[4,104,832]{2,1,0:T(8,128)(2,1)S(1)}, u32[]{:S(2)}, u32[]{:S(2)}) async-start(bf16[4,104,832]{2,1,0:T(8,128)(2,1)} %get-tuple-element.18), calls=%async_computation | async-start | bytes 1490944 | tf_op jit(solution)/shard_map/all_to_all | solution.py:236
  14.6 69.3 %all-gather.3.cloned.1.call-start = ((), (), s32[]{:S(2)}) async-start(), calls=%async_computation.4 | async-start | bytes 7520256 | tf_op jit(solution)/shard_map/all_gather | solution.py:238
  14.6 7.5 %collective-permute-start = (bf16[32,3456]{1,0:T(8,128)(2,1)}, bf16[32,3456]{1,0:T(8,128)(2,1)S(1)}, u32[]{:S(2)}, u32[]{:S(2)}) collective-permute-start(bf16[32,3456]{1,0:T(8,128)(2,1)} %get-tuple-element.17), channel_id=1, source_target_pairs={{0,16},{16,0},{1,17},{17,1},{2,18},{18,2},{3,19},{19,3},{4,20},{20... | collective-permute-start | bytes 663560 | tf_op jit(solution)/shard_map/ppermute | solution.py:136
  24.4 0.8 copy-start.3
  47.9 48.0 %copy-start = (f32[104,208]{1,0:T(8,128)S(1)}, f32[104,208]{1,0:T(8,128)}, u32[]{:S(2)}) copy-start(f32[104,208]{1,0:T(8,128)} %anchor_ref.3) | copy-start | bytes 259588
  47.9 48.0 %copy-start.1 = (f32[104,208]{1,0:T(8,128)S(1)}, f32[104,208]{1,0:T(8,128)}, u32[]{:S(2)}) copy-start(f32[104,208]{1,0:T(8,128)} %momentum_ref.3) | copy-start | bytes 259588
  47.9 0.9 copy-start.2
  50.1 12.2 %all-to-all-start.2 = ((bf16[4,4,104,256]{3,2,1,0:T(8,128)(2,1)}), bf16[4,4,104,256]{3,2,1,0:T(8,128)(2,1)S(1)}, u32[]{:S(2)}, u32[]{:S(2)}) async-start(bf16[4,4,104,256]{3,2,1,0:T(8,128)(2,1)} %get-tuple-element.22), calls=%async_computation.2 | async-start | bytes 1703936 | tf_op jit(solution)/shard_map/all_to_all | solution.py:245
  63.2 32.7 %all-to-all-start.3 = ((f32[128,1,128]{2,1,0:T(1,128)}), f32[128,1,128]{2,1,0:T(1,128)S(1)}, u32[]{:S(2)}, u32[]{:S(2)}) async-start(f32[128,1,128]{2,1,0:T(1,128)} %get-tuple-element.23), calls=%async_computation.3 | async-start | bytes 131072 | tf_op jit(solution)/shard_map/all_to_all | solution.py:249
Sparse Core Ops, SparseCore 0:
  24.6 59.2 all-gather.2

commit v4 on v3

--- a/solution.py
+++ b/solution.py
@@ -17,6 +17,7 @@
 CHUNK = 256
 COLS = 256
 WIDTH = D // 16
+WINDOW = 896
 
 INNER_RATE = 2.0
 INNER_DECAY = 0.1
@@ -136,61 +137,67 @@
     return lax.ppermute(value, axis, [(i, i ^ mask) for i in range(count)])
 
 
-def small_call(kernel, out_shapes, *args, limit=8):
+def small_call(kernel, out_shapes, *args):
     vmem = pl.BlockSpec(memory_space=pltpu.VMEM)
     return pl.pallas_call(
         kernel,
         out_shape=[jax.ShapeDtypeStruct(shape, dtype) for shape, dtype in out_shapes],
         in_specs=[vmem] * len(args),
         out_specs=[vmem] * len(out_shapes),
-        compiler_params=pltpu.CompilerParams(vmem_limit_bytes=limit * 1024 * 1024),
+        compiler_params=pltpu.CompilerParams(vmem_limit_bytes=8 * 1024 * 1024),
     )(*args)
 
 
-def pack_kernel(
-    delta_ref, pool_ref, ids_ref, anchor_ref, momentum_ref, sums_ref, rows_ref, rounded_ref, held_ref
-):
-    rounded_ref[...] = anchor_ref[...].astype(jnp.bfloat16)
-    held_ref[...] = momentum_ref[...]
-    part = D // 4
-    for i in range(4):
-        sums_ref[i] = delta_ref[0, :, i * part : (i + 1) * part]
-    rows_ref[:, :D] = pool_ref[0]
-    ids = ids_ref[0].astype(jnp.float32)
-    square = (BLOCK, BLOCK)
-    diagonal = lax.broadcasted_iota(jnp.int32, square, 0) == lax.broadcasted_iota(jnp.int32, square, 1)
-    lane = lax.broadcasted_iota(jnp.int32, (BLOCK, EXT), 1)
-    extra = jnp.zeros((BLOCK, EXT), jnp.float32)
-    for step in range(2):
-        row = jnp.broadcast_to(ids[step : step + 1], square)
-        column = jnp.sum(jnp.where(diagonal, row, 0.0), axis=1, keepdims=True)
-        extra = jnp.where(lane == step, jnp.broadcast_to(column, extra.shape), extra)
-    rows_ref[:, D:] = extra.astype(jnp.bfloat16)
-
-
-def middle_kernel(sums_ref, anchor_ref, out_ref):
+def window_kernel(delta_hbm, sums_ref, sems):
+    copies = [
+        pltpu.make_async_copy(
+            delta_hbm.at[0, :, pl.ds(i * (D // 4) // 128 * 128, WINDOW)], sums_ref.at[i], sems.at[i]
+        )
+        for i in range(4)
+    ]
+    for copy in copies:
+        copy.start()
+    for copy in copies:
+        copy.wait()
+
+
+def windows(prev_delta):
+    return pl.pallas_call(
+        window_kernel,
+        out_shape=jax.ShapeDtypeStruct((4, ROWS, WINDOW), jnp.bfloat16),
+        in_specs=[pl.BlockSpec(memory_space=pl.ANY)],
+        out_specs=pl.BlockSpec(memory_space=pltpu.VMEM),
+        scratch_shapes=[pltpu.SemaphoreType.DMA((4,))],
+        compiler_params=pltpu.CompilerParams(vmem_limit_bytes=56 * 1024 * 1024),
+    )(prev_delta)
+
+
+def middle_kernel(place_ref, sums_ref, anchor_ref, out_ref):
     sums = sum(sums_ref[i].astype(jnp.float32) for i in range(4))
+    sums = jnp.where(place_ref[1] % 2 == 1, sums[:, WINDOW - D // 4 :], sums[:, : D // 4])
     for i in range(4):
         out_ref[i, 0] = sums[:, i * WIDTH : (i + 1) * WIDTH].astype(jnp.bfloat16)
         out_ref[i, 1] = anchor_ref[...]
 
 
-def square_kernel(mixed_ref, momentum_ref, corrected_ref, out_ref):
+def square_kernel(mixed_ref, stale_ref, corrected_ref, out_ref):
     averaged = sum(mixed_ref[i, 0].astype(jnp.float32) for i in range(4)) / 16
-    corrected = averaged + PENALTY * (averaged - momentum_ref[...])
+    corrected = averaged + (PENALTY * averaged - stale_ref[...])
     corrected_ref[...] = corrected
     squares = jnp.sum(corrected * corrected, axis=(0, 1), keepdims=True)
-    shape = (ROWS, 256 - WIDTH)
+    shape = (ROWS, WINDOW - D // 4)
     lane = lax.broadcasted_iota(jnp.int32, shape, 1)
     squares = jnp.broadcast_to(squares, shape)
     top = squares.astype(jnp.bfloat16).astype(jnp.float32)
     middle = (squares - top).astype(jnp.bfloat16).astype(jnp.float32)
     note = jnp.where(lane == 0, top, jnp.where(lane == 1, middle, squares - top - middle))
     note = jnp.where(lane < 3, note, 0.0).astype(jnp.bfloat16)
+    for j in range(4):
+        block = mixed_ref[j, 1]
+        for i in range(4):
+            out_ref[i, :, j * WIDTH : (j + 1) * WIDTH] = block
     for i in range(4):
-        for j in range(4):
-            out_ref[i, j, :, :WIDTH] = mixed_ref[j, 1]
-            out_ref[i, j, :, WIDTH:] = note
+        out_ref[i, :, D // 4 :] = note
 
 
 def unpack_kernel(blocks_ref, anchor_ref, spread_ref):
@@ -199,11 +206,9 @@
     row = lax.broadcasted_iota(jnp.int32, shape, 0)
     squares = jnp.zeros(shape, jnp.float32)
     for i in range(4):
-        for j in range(4):
-            place = (i * 4 + j) * WIDTH
-            anchor_ref[:, place : place + WIDTH] = blocks_ref[i, j, :, :WIDTH]
-        squares = squares + blocks_ref[i, 0, :, 128:].astype(jnp.float32)
-    squares = jnp.where((row == 0) & (lane >= WIDTH - 128), squares, 0.0)
+        anchor_ref[:, i * (D // 4) : (i + 1) * (D // 4)] = blocks_ref[i, :, : D // 4]
+        squares = squares + blocks_ref[i, :, WINDOW - 128 :].astype(jnp.float32)
+    squares = jnp.where((row == 0) & (lane >= 128 - (WINDOW - D // 4)), squares, 0.0)
     squares = jnp.sum(squares, axis=(0, 1), keepdims=True)
     spread_ref[...] = jnp.broadcast_to(squares.reshape(1, 1, 1), spread_ref.shape)
 
@@ -218,29 +223,36 @@
     new_anchor_ref[...] = anchor_ref[...] - OUTER_RATE * (MOMENT_DECAY * new_momentum + clipped)
 
 
+def middle(place, sums, rounded):
+    vmem = pl.BlockSpec(memory_space=pltpu.VMEM)
+    return pl.pallas_call(
+        middle_kernel,
+        out_shape=[jax.ShapeDtypeStruct((4, 2, ROWS, WIDTH), jnp.bfloat16)],
+        in_specs=[pl.BlockSpec(memory_space=pltpu.SMEM), vmem, vmem],
+        out_specs=[vmem],
+        compiler_params=pltpu.CompilerParams(vmem_limit_bytes=8 * 1024 * 1024),
+    )(place, sums, rounded)
+
+
 def body(anchor, prev_delta, momentum, pool, ids, cotangent):
     tie = lax.optimization_barrier
     bf16, f32 = jnp.bfloat16, jnp.float32
     block = (ROWS, WIDTH)
-    place = lax.axis_index("zl").reshape(1).astype(jnp.int32)
-    sums, rows, rounded, held = small_call(
-        pack_kernel,
-        [((4, ROWS, D // 4), bf16), ((BLOCK, D + EXT), bf16), (block, bf16), (block, f32)],
-        prev_delta,
-        pool,
-        ids,
-        anchor,
-        momentum,
-        limit=56,
-    )
+    place = jnp.stack([lax.axis_index("zl"), lax.axis_index("x")]).astype(jnp.int32)
+    sampled = jnp.pad(ids[0].T.astype(bf16), ((0, 0), (0, EXT - ids.shape[1])))
+    rows = jnp.concatenate([pool[0], sampled], axis=1)
+    other_rows = swap(rows, "zl", 1)
+    sums = windows(prev_delta)
+    rounded = anchor.astype(bf16)
+    stale = PENALTY * momentum
+    other_rows, sums, rounded, stale = tie((other_rows, sums, rounded, stale))
+    gathered = lax.all_gather(jnp.stack([rows, other_rows]), ("y", "c"), axis=0)
+
     sums = lax.all_to_all(sums, "x", 0, 0)
-    other_rows, sums = tie((swap(rows, "zl", 1), sums))
-    gathered = lax.all_gather(jnp.stack([rows, other_rows]), ("y", "c"), axis=0)
-
-    (mixed,) = small_call(middle_kernel, [((4, 2, *block), bf16)], sums, rounded)
+    (mixed,) = middle(place, sums, rounded)
     mixed = lax.all_to_all(mixed, "zh", 0, 0)
     corrected, blocks = small_call(
-        square_kernel, [(block, f32), ((4, 4, ROWS, 256), bf16)], mixed, held
+        square_kernel, [(block, f32), ((4, ROWS, WINDOW), bf16)], mixed, stale
     )
     blocks = lax.all_to_all(blocks, "x", 0, 0)
     anchor_island, spread = small_call(

time: 104 us -> 102 us (0.981)
  blocking collectives: 22.5 us -> 32.2 us
  waiting for transfers between devices: 14.4 us -> 8.09 us
  starting transfers between devices: 31.4 us -> 25.5 us
  other arithmetic: 1.75 us -> 4.39 us
  local copies, waits for them, and re-layouts: 1.75 us -> 0.12 us
    all_to_all x0 -> x1, blocking collectives: none -> 10.6 us  [body(): blocks = lax.all_to_all(blocks, 'x', 0, 0)]
    all_to_all x1 -> x0, waiting for transfers between devices: 8.69 us -> none  [body(): blocks = lax.all_to_all(blocks, 'x', 0, 0)]
    all_to_all x1, waiting for transfers between devices: 0.6 us -> 8.04 us  [body(): sums = lax.all_to_all(sums, 'x', 0, 0)]
    pallas_call x5 -> x3, Pallas kernels: 5.74 us -> 2 us  [small_call(): pl.pallas_call(kernel, out_shape=[jax.ShapeDtypeStruct(shape, dtype) for...]
    all_to_all x1, starting transfers between devices: 19.1 us -> 15.4 us  [body(): spread = lax.all_to_all(spread, ('zh', *FSDP), 0, 0)]
    ppermute x1, waiting for transfers between devices: 3.52 us -> 0.01 us  [swap(): return lax.ppermute(value, axis, [(i, i ^ mask) for i in range(count)])]
    all_to_all x1 -> x0, starting transfers between devices: 3.5 us -> none  [body(): blocks = lax.all_to_all(blocks, 'x', 0, 0)]
    pallas_call x0 -> x2, Pallas kernels: none -> 2.94 us  [the longest x1 2.12 us: windows(): pl.pallas_call(window_kernel, out_shape=jax.ShapeDtypeStruct((4, ROWS, WI...]
  transfers between devices with their start and end apart: 5 -> 4, of which waited for: 4 -> 1; matrix products, arithmetic and copies ran while one was open for 0% -> 2% of each run, Pallas kernels for 14% -> 16%
where the time goes in v4:
time: 102 us
  blocking collectives  32.2 us (32%)
  starting transfers between devices  25.5 us (25%)
  Pallas kernels  17.5 us (17%)
  between operations  14.1 us (14%)
  waiting for transfers between devices  8.09 us (8%)
  other arithmetic  4.39 us (4%)
    all_to_all x1, blocking collectives, body(): mixed = lax.all_to_all(mixed, 'zh', 0, 0)  21.6 us
    all_to_all x1, starting transfers between devices, body(): spread = lax.all_to_all(spread, ('zh', *FSDP), 0, 0)  15.4 us
    pallas_call x1, Pallas kernels, inner_steps(): pl.pallas_call(inner_kernel, out_shape=jax.ShapeDtypeStruct((ROWS, D), jn...  12.5 us
    all_to_all x1, blocking collectives, body(): blocks = lax.all_to_all(blocks, 'x', 0, 0)  10.6 us
    all_to_all x1, waiting for transfers between devices, body(): sums = lax.all_to_all(sums, 'x', 0, 0)  8.04 us
    all_to_all x1, starting transfers between devices, body(): sums = lax.all_to_all(sums, 'x', 0, 0)  5.22 us
    ppermute x1, starting transfers between devices, swap(): return lax.ppermute(value, axis, [(i, i ^ mask) for i in range(count)])  4.83 us
    pallas_call x1, Pallas kernels, windows(): pl.pallas_call(window_kernel, out_shape=jax.ShapeDtypeStruct((4, ROWS, WI...  2.12 us
  transfers between devices with their start and end apart: 4, of which 1 were waited for; matrix products, arithmetic and copies ran while one was open for 2% of the time, Pallas kernels for 16%

profile of v4, /device:TPU:1, one launch (start us, length us, event | category | flops | bytes accessed | tf_op | source)
XLA Modules:
  0.0 102.0 jit_solution(2813208787761297487)
XLA Ops:
  7.2 0.0 copy-start.2
  7.2 0.0 all-gather.3.cloned.1.call-start
  7.2 0.7 convert_bitcast_fusion
  7.9 0.1 copy.11
  8.0 1.0 fusion.2
  9.0 4.8 %collective-permute-start = (bf16[32,3456]{1,0:T(8,128)(2,1)S(1)}, bf16[32,3456]{1,0:T(8,128)(2,1)S(1)}, u32[]{:S(2)}, u32[]{:S(2)}) collective-permute-start(bf16[32,3456]{1,0:T(8,128)(2,1)S(1)} %get-tuple-element.28), channel_id=1, source_target_pairs={{0,16},{16,0},{1,17},{17,1},{2,18},{18,2},{3,19},{19,3},{4,20},{20... | collective-permute-start | bytes 663560 | tf_op jit(solution)/shard_map/ppermute | solution.py:137
  13.9 2.1 %shard_map.85 = bf16[4,104,896]{2,1,0:T(8,128)(2,1)} custom-call(bf16[1,104,3328]{2,1,0:T(8,128)(2,1)} %delta_hbm.1), custom_call_target="tpu_custom_call" | custom-call | tf_op jit(solution)/shard_map/pallas_call | solution.py:165
  16.0 0.9 convert_element_type.17.anchor_ref
  16.9 0.9 broadcast_multiply_fusion.stale_ref
  17.8 0.0 collective-permute-done
  17.8 0.8 pad_maximum_fusion
  18.6 0.0 all-gather.3.cloned.1.call-update
  18.6 5.2 %all-to-all-start = ((bf16[4,104,896]{2,1,0:T(8,128)(2,1)}), bf16[4,104,896]{2,1,0:T(8,128)(2,1)S(1)}, u32[]{:S(2)}, u32[]{:S(2)}) async-start(bf16[4,104,896]{2,1,0:T(8,128)(2,1)} %shard_map.85), calls=%async_computation | async-start | bytes 1490944 | tf_op jit(solution)/shard_map/all_to_all | solution.py:251
  23.9 0.1 pad_add_fusion.place_ref
  23.9 8.0 %all-to-all-done.sums_ref = bf16[4,104,896]{2,1,0:T(8,128)(2,1)S(1)} async-done(((bf16[4,104,896]{2,1,0:T(8,128)(2,1)}), bf16[4,104,896]{2,1,0:T(8,128)(2,1)S(1)}, u32[]{:S(2)}, u32[]{:S(2)}) %all-to-all-start) | async-done | bytes 745504 | tf_op jit(solution)/shard_map/all_to_all | solution.py:251
  32.0 0.8 shard_map.86
  32.8 0.0 copy-start
  32.8 0.0 copy-start.1
  32.8 21.6 %all_to_all.20.mixed_ref = bf16[4,2,104,208]{3,2,1,0:T(8,128)(2,1)S(1)} all-to-all(bf16[4,2,104,208]{3,2,1,0:T(8,128)(2,1)S(1)} %shard_map.86), channel_id=1, replica_groups=mesh['x'=4,'zh'=4,'zl'=2,'y'=8,'c'=2] {'zh'}, dimensions={0} | all-to-all | bytes 692224 | tf_op jit(solution)/shard_map/all_to_all | solution.py:253
  54.5 0.3 shard_map.87
  54.8 10.6 %all_to_all.21.blocks_ref = bf16[4,104,896]{2,1,0:T(8,128)(2,1)S(1)} all-to-all(bf16[4,104,896]{2,1,0:T(8,128)(2,1)S(1)} %get-tuple-element.18), channel_id=1, replica_groups=mesh['x'=4,'zh'=4,'zl'=2,'y'=8,'c'=2] {'x'}, dimensions={0} | all-to-all | bytes 1490944 | tf_op jit(solution)/shard_map/all_to_all | solution.py:257
  65.3 0.8 shard_map.88
  66.2 15.4 %all-to-all-start.3 = ((f32[128,1,128]{2,1,0:T(1,128)}), f32[128,1,128]{2,1,0:T(1,128)S(1)}, u32[]{:S(2)}, u32[]{:S(2)}) async-start(f32[128,1,128]{2,1,0:T(1,128)} %get-tuple-element.19), calls=%async_computation.3 | async-start | bytes 131072 | tf_op jit(solution)/shard_map/all_to_all | solution.py:261
  81.6 0.0 all-gather.3.cloned.1.call-done
  81.6 0.0 copy-done.2
  81.6 12.5 %shard_map.89 = bf16[104,3328]{1,0:T(8,128)(2,1)} custom-call(s32[2]{0:T(128)S(1)} %pad_add_fusion.place_ref, bf16[104,3328]{1,0:T(8,128)(2,1)S(1)} %get-tuple-element.20.anchor_ref, bf16[2,104,1024]{2,1,0:T(8,128)(2,1)S(1)} %bitcast.13, bf16[16,2,32,3456]{3,2,1,0:T(8,128)(2,1)} %bitcast.16), custom_call_target="tpu_custom_call" | custom-call | flops 2835349504 | bytes 9000000 | tf_op jit(solution)/shard_map/pallas_call | solution.py:111
  94.2 0.0 all-to-all-done.3.spread_ref
  94.2 0.0 copy-done
  94.2 0.0 copy-done.1
  94.2 0.9 shard_map.90
Async XLA Ops:
  7.2 74.5 %copy-start.2 = (bf16[1,2,104,1024]{3,2,1,0:T(8,128)(2,1)S(1)}, bf16[1,2,104,1024]{3,2,1,0:T(8,128)(2,1)}, u32[]{:S(2)}) copy-start(bf16[1,2,104,1024]{3,2,1,0:T(8,128)(2,1)} %param.11) | copy-start | bytes 1277956
  7.2 74.5 %all-gather.3.cloned.1.call-start = ((), (), s32[]{:S(2)}) async-start(), calls=%async_computation.4 | async-start | bytes 7520256 | tf_op jit(solution)/shard_map/all_gather | solution.py:249
  9.0 8.8 %collective-permute-start = (bf16[32,3456]{1,0:T(8,128)(2,1)S(1)}, bf16[32,3456]{1,0:T(8,128)(2,1)S(1)}, u32[]{:S(2)}, u32[]{:S(2)}) collective-permute-start(bf16[32,3456]{1,0:T(8,128)(2,1)S(1)} %get-tuple-element.28), channel_id=1, source_target_pairs={{0,16},{16,0},{1,17},{17,1},{2,18},{18,2},{3,19},{19,3},{4,20},{20... | collective-permute-start | bytes 663560 | tf_op jit(solution)/shard_map/ppermute | solution.py:137
  18.6 13.3 %all-to-all-start = ((bf16[4,104,896]{2,1,0:T(8,128)(2,1)}), bf16[4,104,896]{2,1,0:T(8,128)(2,1)S(1)}, u32[]{:S(2)}, u32[]{:S(2)}) async-start(bf16[4,104,896]{2,1,0:T(8,128)(2,1)} %shard_map.85), calls=%async_computation | async-start | bytes 1490944 | tf_op jit(solution)/shard_map/all_to_all | solution.py:251
  32.8 61.4 %copy-start = (f32[104,208]{1,0:T(8,128)S(1)}, f32[104,208]{1,0:T(8,128)}, u32[]{:S(2)}) copy-start(f32[104,208]{1,0:T(8,128)} %anchor_ref.1) | copy-start | bytes 259588
  32.8 61.4 %copy-start.1 = (f32[104,208]{1,0:T(8,128)S(1)}, f32[104,208]{1,0:T(8,128)}, u32[]{:S(2)}) copy-start(f32[104,208]{1,0:T(8,128)} %momentum_ref.1) | copy-start | bytes 259588
  66.2 28.1 %all-to-all-start.3 = ((f32[128,1,128]{2,1,0:T(1,128)}), f32[128,1,128]{2,1,0:T(1,128)S(1)}, u32[]{:S(2)}, u32[]{:S(2)}) async-start(f32[128,1,128]{2,1,0:T(1,128)} %get-tuple-element.19), calls=%async_computation.3 | async-start | bytes 131072 | tf_op jit(solution)/shard_map/all_to_all | solution.py:261
Sparse Core Ops, SparseCore 0:
  18.8 58.2 all-gather.2

commit v5 on v4

--- a/solution.py
+++ b/solution.py
@@ -231,6 +231,7 @@
         in_specs=[pl.BlockSpec(memory_space=pltpu.SMEM), vmem, vmem],
         out_specs=[vmem],
         compiler_params=pltpu.CompilerParams(vmem_limit_bytes=8 * 1024 * 1024),
+        cost_estimate=pl.CostEstimate(flops=200000000000, bytes_accessed=1_000_000, transcendentals=0),
     )(place, sums, rounded)
 
 
@@ -239,14 +240,14 @@
     bf16, f32 = jnp.bfloat16, jnp.float32
     block = (ROWS, WIDTH)
     place = jnp.stack([lax.axis_index("zl"), lax.axis_index("x")]).astype(jnp.int32)
-    sampled = jnp.pad(ids[0].T.astype(bf16), ((0, 0), (0, EXT - ids.shape[1])))
+    sampled = jnp.pad(ids[0].T, ((0, 0), (0, EXT - ids.shape[1]))).astype(bf16)
     rows = jnp.concatenate([pool[0], sampled], axis=1)
     other_rows = swap(rows, "zl", 1)
     sums = windows(prev_delta)
-    rounded = anchor.astype(bf16)
-    stale = PENALTY * momentum
-    other_rows, sums, rounded, stale = tie((other_rows, sums, rounded, stale))
-    gathered = lax.all_gather(jnp.stack([rows, other_rows]), ("y", "c"), axis=0)
+    pairs, held_anchor, held_momentum = tie((jnp.stack([rows, other_rows]), anchor, momentum))
+    gathered = lax.all_gather(pairs, ("y", "c"), axis=0)
+    rounded = held_anchor.astype(bf16)
+    stale = PENALTY * held_momentum
 
     sums = lax.all_to_all(sums, "x", 0, 0)
     (mixed,) = middle(place, sums, rounded)

time: 102 us -> 102 us (level)
  blocking collectives: 32.2 us -> 11.4 us
  starting transfers between devices: 25.5 us -> 36.1 us
  waiting for transfers between devices: 8.09 us -> 17.7 us
    all_to_all x1 -> x0, blocking collectives: 21.6 us -> none  [body(): mixed = lax.all_to_all(mixed, 'zh', 0, 0)]
    all_to_all x0 -> x1, starting transfers between devices: none -> 11.7 us  [body(): mixed = lax.all_to_all(mixed, 'zh', 0, 0)]
    all_to_all x0 -> x1, waiting for transfers between devices: none -> 11.3 us  [body(): mixed = lax.all_to_all(mixed, 'zh', 0, 0)]
    all_to_all x1, waiting for transfers between devices: 8.04 us -> 6.35 us  [body(): sums = lax.all_to_all(sums, 'x', 0, 0)]
    all_to_all x1, starting transfers between devices: 5.22 us -> 4.02 us  [body(): sums = lax.all_to_all(sums, 'x', 0, 0)]
  transfers between devices with their start and end apart: 4 -> 5, of which waited for: 1 -> 2; matrix products, arithmetic and copies ran while one was open for 2% -> 2% of each run, Pallas kernels for 16% -> 17%
where the time goes in v5:
time: 102 us; the launch traced here: 101 us
  starting transfers between devices  36.1 us (35%)
  Pallas kernels  18.2 us (18%)
  waiting for transfers between devices  17.7 us (17%)
  between operations  14.1 us (14%)
  blocking collectives  11.4 us (11%)
  other arithmetic  3.45 us (3%)
    all_to_all x1, starting transfers between devices, body(): spread = lax.all_to_all(spread, ('zh', *FSDP), 0, 0)  15.6 us
    pallas_call x1, Pallas kernels, inner_steps(): pl.pallas_call(inner_kernel, out_shape=jax.ShapeDtypeStruct((ROWS, D), jn...  12.6 us
    all_to_all x1, starting transfers between devices, body(): mixed = lax.all_to_all(mixed, 'zh', 0, 0)  11.7 us
    all_to_all x1, blocking collectives, body(): blocks = lax.all_to_all(blocks, 'x', 0, 0)  11.4 us
    all_to_all x1, waiting for transfers between devices, body(): mixed = lax.all_to_all(mixed, 'zh', 0, 0)  11.3 us
    all_to_all x1, waiting for transfers between devices, body(): sums = lax.all_to_all(sums, 'x', 0, 0)  6.35 us
    ppermute x1, starting transfers between devices, swap(): return lax.ppermute(value, axis, [(i, i ^ mask) for i in range(count)])  4.83 us
    all_to_all x1, starting transfers between devices, body(): sums = lax.all_to_all(sums, 'x', 0, 0)  4.02 us
  transfers between devices with their start and end apart: 5, of which 2 were waited for; matrix products, arithmetic and copies ran while one was open for 2% of the time, Pallas kernels for 17%

profile of v5, /device:TPU:1, one launch (start us, length us, event | category | flops | bytes accessed | tf_op | source)
XLA Modules:
  0.0 101.1 jit_solution(11713026588728028848)
XLA Ops:
  7.2 0.7 convert_bitcast_fusion
  7.8 0.1 copy.11
  8.0 1.0 fusion.2
  8.9 4.8 %collective-permute-start = (bf16[32,3456]{1,0:T(8,128)(2,1)S(1)}, bf16[32,3456]{1,0:T(8,128)(2,1)S(1)}, u32[]{:S(2)}, u32[]{:S(2)}) collective-permute-start(bf16[32,3456]{1,0:T(8,128)(2,1)S(1)} %get-tuple-element.26), channel_id=1, source_target_pairs={{0,16},{16,0},{1,17},{17,1},{2,18},{18,2},{3,19},{19,3},{4,20},{20... | collective-permute-start | bytes 663560 | tf_op jit(solution)/shard_map/ppermute | solution.py:137
  13.8 2.1 %shard_map.85 = bf16[4,104,896]{2,1,0:T(8,128)(2,1)} custom-call(bf16[1,104,3328]{2,1,0:T(8,128)(2,1)} %delta_hbm.1), custom_call_target="tpu_custom_call" | custom-call | tf_op jit(solution)/shard_map/pallas_call | solution.py:165
  15.9 4.0 %all-to-all-start = ((bf16[4,104,896]{2,1,0:T(8,128)(2,1)}), bf16[4,104,896]{2,1,0:T(8,128)(2,1)S(1)}, u32[]{:S(2)}, u32[]{:S(2)}) async-start(bf16[4,104,896]{2,1,0:T(8,128)(2,1)} %shard_map.85), calls=%async_computation | async-start | bytes 1490944 | tf_op jit(solution)/shard_map/all_to_all | solution.py:252
  19.9 0.0 all-gather.3.cloned.1.call-start
  19.9 0.1 pad_add_fusion.place_ref
  20.0 0.0 collective-permute-done
  20.0 0.8 pad_maximum_fusion
  20.8 0.9 convert_element_type.4.anchor_ref
  21.7 0.0 all-gather.3.cloned.1.call-update
  21.7 6.3 %all-to-all-done.sums_ref = bf16[4,104,896]{2,1,0:T(8,128)(2,1)S(1)} async-done(((bf16[4,104,896]{2,1,0:T(8,128)(2,1)}), bf16[4,104,896]{2,1,0:T(8,128)(2,1)S(1)}, u32[]{:S(2)}, u32[]{:S(2)}) %all-to-all-start) | async-done | bytes 745504 | tf_op jit(solution)/shard_map/all_to_all | solution.py:252
  28.1 0.0 copy-start.1
  28.1 0.0 copy-start.2
  28.1 1.6 %shard_map.86 = bf16[4,2,104,208]{3,2,1,0:T(8,128)(2,1)} custom-call(s32[2]{0:T(128)S(1)} %pad_add_fusion.place_ref, bf16[4,104,896]{2,1,0:T(8,128)(2,1)S(1)} %all-to-all-done.sums_ref, bf16[104,208]{1,0:T(8,128)(2,1)S(1)} %convert_element_type.4.anchor_ref), custom_call_target="tpu_custom_call" | custom-call | flops 199999995904 | bytes 1000000 | tf_op jit(solution)/shard_map/pallas_call | solution.py:228
  29.6 0.0 copy-start
  29.6 11.7 %all-to-all-start.1 = ((bf16[4,2,104,208]{3,2,1,0:T(8,128)(2,1)}), bf16[4,2,104,208]{3,2,1,0:T(8,128)(2,1)S(1)}, u32[]{:S(2)}, u32[]{:S(2)}) async-start(bf16[4,2,104,208]{3,2,1,0:T(8,128)(2,1)} %shard_map.86), calls=%async_computation.1 | async-start | bytes 851968 | tf_op jit(solution)/shard_map/all_to_all | solution.py:254
  41.4 0.0 copy-done.1
  41.4 11.3 %all-to-all-done.1.mixed_ref = bf16[4,2,104,208]{3,2,1,0:T(8,128)(2,1)S(1)} async-done(((bf16[4,2,104,208]{3,2,1,0:T(8,128)(2,1)}), bf16[4,2,104,208]{3,2,1,0:T(8,128)(2,1)S(1)}, u32[]{:S(2)}, u32[]{:S(2)}) %all-to-all-start.1) | async-done | bytes 346144 | tf_op jit(solution)/shard_map/all_to_all | solution.py:254
  52.7 0.3 shard_map.87
  53.0 11.4 %all_to_all.20.blocks_ref = bf16[4,104,896]{2,1,0:T(8,128)(2,1)S(1)} all-to-all(bf16[4,104,896]{2,1,0:T(8,128)(2,1)S(1)} %get-tuple-element.16), channel_id=1, replica_groups=mesh['x'=4,'zh'=4,'zl'=2,'y'=8,'c'=2] {'x'}, dimensions={0} | all-to-all | bytes 1490944 | tf_op jit(solution)/shard_map/all_to_all | solution.py:258
  64.3 0.8 shard_map.88
  65.2 15.6 %all-to-all-start.3 = ((f32[128,1,128]{2,1,0:T(1,128)}), f32[128,1,128]{2,1,0:T(1,128)S(1)}, u32[]{:S(2)}, u32[]{:S(2)}) async-start(f32[128,1,128]{2,1,0:T(1,128)} %get-tuple-element.17), calls=%async_computation.3 | async-start | bytes 131072 | tf_op jit(solution)/shard_map/all_to_all | solution.py:262
  80.7 0.0 all-gather.3.cloned.1.call-done
  80.8 0.0 copy-done.2
  80.8 12.6 %shard_map.89 = bf16[104,3328]{1,0:T(8,128)(2,1)} custom-call(s32[2]{0:T(128)S(1)} %pad_add_fusion.place_ref, bf16[104,3328]{1,0:T(8,128)(2,1)S(1)} %get-tuple-element.18.anchor_ref, bf16[2,104,1024]{2,1,0:T(8,128)(2,1)S(1)} %bitcast.13, bf16[16,2,32,3456]{3,2,1,0:T(8,128)(2,1)} %bitcast.16), custom_call_target="tpu_custom_call" | custom-call | flops 2835349504 | bytes 9000000 | tf_op jit(solution)/shard_map/pallas_call | solution.py:111
  93.3 0.0 all-to-all-done.3.spread_ref
  93.3 0.0 copy-done
  93.3 0.9 shard_map.90
  (1 shorter events, 0.0 us)
Async XLA Ops:
  8.9 11.1 %collective-permute-start = (bf16[32,3456]{1,0:T(8,128)(2,1)S(1)}, bf16[32,3456]{1,0:T(8,128)(2,1)S(1)}, u32[]{:S(2)}, u32[]{:S(2)}) collective-permute-start(bf16[32,3456]{1,0:T(8,128)(2,1)S(1)} %get-tuple-element.26), channel_id=1, source_target_pairs={{0,16},{16,0},{1,17},{17,1},{2,18},{18,2},{3,19},{19,3},{4,20},{20... | collective-permute-start | bytes 663560 | tf_op jit(solution)/shard_map/ppermute | solution.py:137
  15.9 12.2 %all-to-all-start = ((bf16[4,104,896]{2,1,0:T(8,128)(2,1)}), bf16[4,104,896]{2,1,0:T(8,128)(2,1)S(1)}, u32[]{:S(2)}, u32[]{:S(2)}) async-start(bf16[4,104,896]{2,1,0:T(8,128)(2,1)} %shard_map.85), calls=%async_computation | async-start | bytes 1490944 | tf_op jit(solution)/shard_map/all_to_all | solution.py:252
  19.9 60.9 %all-gather.3.cloned.1.call-start = ((), (), s32[]{:S(2)}) async-start(), calls=%async_computation.4 | async-start | bytes 7520256 | tf_op jit(solution)/shard_map/all_gather | solution.py:248
  28.1 13.3 %copy-start.1 = (f32[104,208]{1,0:T(8,128)S(1)}, f32[104,208]{1,0:T(8,128)}, u32[]{:S(2)}) copy-start(f32[104,208]{1,0:T(8,128)} %momentum_ref.1) | copy-start | bytes 259588
  28.1 52.7 %copy-start.2 = (bf16[1,2,104,1024]{3,2,1,0:T(8,128)(2,1)S(1)}, bf16[1,2,104,1024]{3,2,1,0:T(8,128)(2,1)}, u32[]{:S(2)}) copy-start(bf16[1,2,104,1024]{3,2,1,0:T(8,128)(2,1)} %param.11) | copy-start | bytes 1277956
  29.6 63.7 %copy-start = (f32[104,208]{1,0:T(8,128)S(1)}, f32[104,208]{1,0:T(8,128)}, u32[]{:S(2)}) copy-start(f32[104,208]{1,0:T(8,128)} %anchor_ref.1) | copy-start | bytes 259588
  29.6 23.0 %all-to-all-start.1 = ((bf16[4,2,104,208]{3,2,1,0:T(8,128)(2,1)}), bf16[4,2,104,208]{3,2,1,0:T(8,128)(2,1)S(1)}, u32[]{:S(2)}, u32[]{:S(2)}) async-start(bf16[4,2,104,208]{3,2,1,0:T(8,128)(2,1)} %shard_map.86), calls=%async_computation.1 | async-start | bytes 851968 | tf_op jit(solution)/shard_map/all_to_all | solution.py:254
  65.2 28.2 %all-to-all-start.3 = ((f32[128,1,128]{2,1,0:T(1,128)}), f32[128,1,128]{2,1,0:T(1,128)S(1)}, u32[]{:S(2)}, u32[]{:S(2)}) async-start(f32[128,1,128]{2,1,0:T(1,128)} %get-tuple-element.17), calls=%async_computation.3 | async-start | bytes 131072 | tf_op jit(solution)/shard_map/all_to_all | solution.py:262
Sparse Core Ops, SparseCore 0:
  23.4 57.2 all-gather.2

commit v6 on v5

--- a/solution.py
+++ b/solution.py
@@ -69,7 +69,7 @@
         picked = picks(chunk, step)
         tokens = slice(chunk * CHUNK, (chunk + 1) * CHUNK)
         preact = jnp.zeros((ROWS, CHUNK), jnp.float32)
-        for _ in range(3):
+        for _ in range(2):
             top = values.astype(jnp.bfloat16)
             values = values - top.astype(jnp.float32)
             preact = preact + lax.dot_general(
@@ -250,6 +250,7 @@
     stale = PENALTY * held_momentum
 
     sums = lax.all_to_all(sums, "x", 0, 0)
+    sums, rounded, stale = tie((sums, rounded, stale))
     (mixed,) = middle(place, sums, rounded)
     mixed = lax.all_to_all(mixed, "zh", 0, 0)
     corrected, blocks = small_call(

time: 102 us -> 101 us (level)
  blocking collectives: 11.4 us -> 33.6 us
  waiting for transfers between devices: 17.7 us -> 5.48 us
  starting transfers between devices: 36.1 us -> 26 us
    all_to_all x0 -> x1, blocking collectives: none -> 23.1 us  [body(): mixed = lax.all_to_all(mixed, 'zh', 0, 0)]
    all_to_all x1 -> x0, starting transfers between devices: 11.7 us -> none  [body(): mixed = lax.all_to_all(mixed, 'zh', 0, 0)]
    all_to_all x1 -> x0, waiting for transfers between devices: 11.3 us -> none  [body(): mixed = lax.all_to_all(mixed, 'zh', 0, 0)]
    all_to_all x1, starting transfers between devices: 15.6 us -> 17.1 us  [body(): spread = lax.all_to_all(spread, ('zh', *FSDP), 0, 0)]
  transfers between devices with their start and end apart: 5 -> 4, of which waited for: 2 -> 1; matrix products, arithmetic and copies ran while one was open for 2% -> 3% of each run, Pallas kernels for 17% -> 16%
where the time goes in v6:
time: 101 us
  blocking collectives  33.6 us (33%)
  starting transfers between devices  26 us (26%)
  Pallas kernels  17.2 us (17%)
  between operations  14.1 us (14%)
  waiting for transfers between devices  5.48 us (5%)
  other arithmetic  4.34 us (4%)
    all_to_all x1, blocking collectives, body(): mixed = lax.all_to_all(mixed, 'zh', 0, 0)  23.1 us
    all_to_all x1, starting transfers between devices, body(): spread = lax.all_to_all(spread, ('zh', *FSDP), 0, 0)  17.1 us
    pallas_call x1, Pallas kernels, inner_steps(): pl.pallas_call(inner_kernel, out_shape=jax.ShapeDtypeStruct((ROWS, D), jn...  12.3 us
    all_to_all x1, blocking collectives, body(): blocks = lax.all_to_all(blocks, 'x', 0, 0)  10.6 us
    all_to_all x1, waiting for transfers between devices, body(): sums = lax.all_to_all(sums, 'x', 0, 0)  5.44 us
    ppermute x1, starting transfers between devices, swap(): return lax.ppermute(value, axis, [(i, i ^ mask) for i in range(count)])  4.83 us
    all_to_all x1, starting transfers between devices, body(): sums = lax.all_to_all(sums, 'x', 0, 0)  4.02 us
    pallas_call x1, Pallas kernels, windows(): pl.pallas_call(window_kernel, out_shape=jax.ShapeDtypeStruct((4, ROWS, WI...  2.12 us
  transfers between devices with their start and end apart: 4, of which 1 were waited for; matrix products, arithmetic and copies ran while one was open for 3% of the time, Pallas kernels for 16%

profile of v6, /device:TPU:1, one launch (start us, length us, event | category | flops | bytes accessed | tf_op | source)
XLA Modules:
  0.0 100.9 jit_solution(2492602258835846976)
XLA Ops:
  7.2 0.7 convert_bitcast_fusion
  7.8 0.1 copy.11
  8.0 1.0 fusion.2
  8.9 4.8 %collective-permute-start = (bf16[32,3456]{1,0:T(8,128)(2,1)S(1)}, bf16[32,3456]{1,0:T(8,128)(2,1)S(1)}, u32[]{:S(2)}, u32[]{:S(2)}) collective-permute-start(bf16[32,3456]{1,0:T(8,128)(2,1)S(1)} %get-tuple-element.32), channel_id=1, source_target_pairs={{0,16},{16,0},{1,17},{17,1},{2,18},{18,2},{3,19},{19,3},{4,20},{20... | collective-permute-start | bytes 663560 | tf_op jit(solution)/shard_map/ppermute | solution.py:137
  13.8 2.1 %shard_map.85 = bf16[4,104,896]{2,1,0:T(8,128)(2,1)} custom-call(bf16[1,104,3328]{2,1,0:T(8,128)(2,1)} %delta_hbm.1), custom_call_target="tpu_custom_call" | custom-call | tf_op jit(solution)/shard_map/pallas_call | solution.py:165
  15.9 4.0 %all-to-all-start = ((bf16[4,104,896]{2,1,0:T(8,128)(2,1)}), bf16[4,104,896]{2,1,0:T(8,128)(2,1)S(1)}, u32[]{:S(2)}, u32[]{:S(2)}) async-start(bf16[4,104,896]{2,1,0:T(8,128)(2,1)} %shard_map.85), calls=%async_computation | async-start | bytes 1490944 | tf_op jit(solution)/shard_map/all_to_all | solution.py:252
  19.9 0.0 all-gather.3.cloned.1.call-start
  19.9 0.1 pad_add_fusion.place_ref
  20.0 0.0 collective-permute-done
  20.0 0.8 pad_maximum_fusion
  20.8 0.9 convert_element_type.4.anchor_ref
  21.7 0.0 all-gather.3.cloned.1.call-update
  21.7 0.9 broadcast_multiply_fusion.stale_ref
  22.6 5.4 %all-to-all-done.sums_ref = bf16[4,104,896]{2,1,0:T(8,128)(2,1)S(1)} async-done(((bf16[4,104,896]{2,1,0:T(8,128)(2,1)}), bf16[4,104,896]{2,1,0:T(8,128)(2,1)S(1)}, u32[]{:S(2)}, u32[]{:S(2)}) %all-to-all-start) | async-done | bytes 745504 | tf_op jit(solution)/shard_map/all_to_all | solution.py:252
  28.1 0.0 copy-start.2
  28.1 0.8 shard_map.86
  28.9 0.0 copy-start
  28.9 0.0 copy-start.1
  28.9 23.1 %all_to_all.20.mixed_ref = bf16[4,2,104,208]{3,2,1,0:T(8,128)(2,1)S(1)} all-to-all(bf16[4,2,104,208]{3,2,1,0:T(8,128)(2,1)S(1)} %shard_map.86), channel_id=1, replica_groups=mesh['x'=4,'zh'=4,'zl'=2,'y'=8,'c'=2] {'zh'}, dimensions={0} | all-to-all | bytes 692224 | tf_op jit(solution)/shard_map/all_to_all | solution.py:255
  52.0 0.3 shard_map.87
  52.3 10.6 %all_to_all.21.blocks_ref = bf16[4,104,896]{2,1,0:T(8,128)(2,1)S(1)} all-to-all(bf16[4,104,896]{2,1,0:T(8,128)(2,1)S(1)} %get-tuple-element.22), channel_id=1, replica_groups=mesh['x'=4,'zh'=4,'zl'=2,'y'=8,'c'=2] {'x'}, dimensions={0} | all-to-all | bytes 1490944 | tf_op jit(solution)/shard_map/all_to_all | solution.py:259
  62.9 0.8 shard_map.88
  63.7 17.1 %all-to-all-start.3 = ((f32[128,1,128]{2,1,0:T(1,128)}), f32[128,1,128]{2,1,0:T(1,128)S(1)}, u32[]{:S(2)}, u32[]{:S(2)}) async-start(f32[128,1,128]{2,1,0:T(1,128)} %get-tuple-element.23), calls=%async_computation.3 | async-start | bytes 131072 | tf_op jit(solution)/shard_map/all_to_all | solution.py:263
  80.8 0.0 all-gather.3.cloned.1.call-done
  80.8 0.0 copy-done.2
  80.8 12.3 %shard_map.89 = bf16[104,3328]{1,0:T(8,128)(2,1)} custom-call(s32[2]{0:T(128)S(1)} %pad_add_fusion.place_ref, bf16[104,3328]{1,0:T(8,128)(2,1)S(1)} %get-tuple-element.24.anchor_ref, bf16[2,104,1024]{2,1,0:T(8,128)(2,1)S(1)} %bitcast.13, bf16[16,2,32,3456]{3,2,1,0:T(8,128)(2,1)} %bitcast.16), custom_call_target="tpu_custom_call" | custom-call | flops 2835349504 | bytes 9000000 | tf_op jit(solution)/shard_map/pallas_call | solution.py:111
  93.1 0.0 all-to-all-done.3.spread_ref
  93.1 0.0 copy-done
  93.1 0.0 copy-done.1
  93.1 0.9 shard_map.90
Async XLA Ops:
  8.9 11.1 %collective-permute-start = (bf16[32,3456]{1,0:T(8,128)(2,1)S(1)}, bf16[32,3456]{1,0:T(8,128)(2,1)S(1)}, u32[]{:S(2)}, u32[]{:S(2)}) collective-permute-start(bf16[32,3456]{1,0:T(8,128)(2,1)S(1)} %get-tuple-element.32), channel_id=1, source_target_pairs={{0,16},{16,0},{1,17},{17,1},{2,18},{18,2},{3,19},{19,3},{4,20},{20... | collective-permute-start | bytes 663560 | tf_op jit(solution)/shard_map/ppermute | solution.py:137
  15.9 12.2 %all-to-all-start = ((bf16[4,104,896]{2,1,0:T(8,128)(2,1)}), bf16[4,104,896]{2,1,0:T(8,128)(2,1)S(1)}, u32[]{:S(2)}, u32[]{:S(2)}) async-start(bf16[4,104,896]{2,1,0:T(8,128)(2,1)} %shard_map.85), calls=%async_computation | async-start | bytes 1490944 | tf_op jit(solution)/shard_map/all_to_all | solution.py:252
  19.9 60.9 %all-gather.3.cloned.1.call-start = ((), (), s32[]{:S(2)}) async-start(), calls=%async_computation.4 | async-start | bytes 7520256 | tf_op jit(solution)/shard_map/all_gather | solution.py:248
  28.1 52.8 %copy-start.2 = (bf16[1,2,104,1024]{3,2,1,0:T(8,128)(2,1)S(1)}, bf16[1,2,104,1024]{3,2,1,0:T(8,128)(2,1)}, u32[]{:S(2)}) copy-start(bf16[1,2,104,1024]{3,2,1,0:T(8,128)(2,1)} %param.11) | copy-start | bytes 1277956
  28.9 64.2 %copy-start = (f32[104,208]{1,0:T(8,128)S(1)}, f32[104,208]{1,0:T(8,128)}, u32[]{:S(2)}) copy-start(f32[104,208]{1,0:T(8,128)} %anchor_ref.1) | copy-start | bytes 259588
  28.9 64.2 %copy-start.1 = (f32[104,208]{1,0:T(8,128)S(1)}, f32[104,208]{1,0:T(8,128)}, u32[]{:S(2)}) copy-start(f32[104,208]{1,0:T(8,128)} %momentum_ref.1) | copy-start | bytes 259588
  63.7 29.4 %all-to-all-start.3 = ((f32[128,1,128]{2,1,0:T(1,128)}), f32[128,1,128]{2,1,0:T(1,128)S(1)}, u32[]{:S(2)}, u32[]{:S(2)}) async-start(f32[128,1,128]{2,1,0:T(1,128)} %get-tuple-element.23), calls=%async_computation.3 | async-start | bytes 131072 | tf_op jit(solution)/shard_map/all_to_all | solution.py:263
Sparse Core Ops, SparseCore 0:
  23.4 57.2 all-gather.2

commit v7 on v6

--- a/solution.py
+++ b/solution.py
@@ -90,11 +90,14 @@
         fold(TOK // CHUNK - 1, step, values)
         for start in range(0, D, COLS):
             cols = slice(start, start + COLS)
-            gradient = jnp.dot(
-                folded[...],
-                pool[:, :, :, cols].reshape(TOK, COLS),
-                preferred_element_type=jnp.float32,
-            )
+            tile = pool[:, :, :, cols].reshape(TOK, COLS)
+            if start == 0:
+                early = TOK - CHUNK
+                gradient = jnp.dot(
+                    folded[:, :early], tile[:early], preferred_element_type=jnp.float32
+                ) + jnp.dot(folded[:, early:], tile[early:], preferred_element_type=jnp.float32)
+            else:
+                gradient = jnp.dot(folded[...], tile, preferred_element_type=jnp.float32)
             before = anchor_ref[:, cols].astype(jnp.float32)
             if step == 0:
                 after = before - INNER_RATE * (gradient / root_width) - INNER_DECAY * before

time: 101 us -> 102 us (level)
  no operation moved by 1% of the time
where the time goes in v7:
time: 102 us; the launch traced here: 101 us
  blocking collectives  33.6 us (33%)
  starting transfers between devices  26 us (25%)
  Pallas kernels  17.5 us (17%)
  between operations  14.1 us (14%)
  waiting for transfers between devices  5.48 us (5%)
  other arithmetic  4.34 us (4%)
    all_to_all x1, blocking collectives, body(): mixed = lax.all_to_all(mixed, 'zh', 0, 0)  23.1 us
    all_to_all x1, starting transfers between devices, body(): spread = lax.all_to_all(spread, ('zh', *FSDP), 0, 0)  17.1 us
    pallas_call x1, Pallas kernels, inner_steps(): pl.pallas_call(inner_kernel, out_shape=jax.ShapeDtypeStruct((ROWS, D), jn...  12.5 us
    all_to_all x1, blocking collectives, body(): blocks = lax.all_to_all(blocks, 'x', 0, 0)  10.6 us
    all_to_all x1, waiting for transfers between devices, body(): sums = lax.all_to_all(sums, 'x', 0, 0)  5.44 us
    ppermute x1, starting transfers between devices, swap(): return lax.ppermute(value, axis, [(i, i ^ mask) for i in range(count)])  4.83 us
    all_to_all x1, starting transfers between devices, body(): sums = lax.all_to_all(sums, 'x', 0, 0)  4.02 us
    pallas_call x1, Pallas kernels, windows(): pl.pallas_call(window_kernel, out_shape=jax.ShapeDtypeStruct((4, ROWS, WI...  2.12 us
  transfers between devices with their start and end apart: 4, of which 1 were waited for; matrix products, arithmetic and copies ran while one was open for 3% of the time, Pallas kernels for 16%

profile of v7, /device:TPU:1, one launch (start us, length us, event | category | flops | bytes accessed | tf_op | source)
XLA Modules:
  0.0 101.1 jit_solution(9960817422146623704)
XLA Ops:
  7.2 0.7 convert_bitcast_fusion
  7.8 0.1 copy.11
  8.0 1.0 fusion.2
  8.9 4.8 %collective-permute-start = (bf16[32,3456]{1,0:T(8,128)(2,1)S(1)}, bf16[32,3456]{1,0:T(8,128)(2,1)S(1)}, u32[]{:S(2)}, u32[]{:S(2)}) collective-permute-start(bf16[32,3456]{1,0:T(8,128)(2,1)S(1)} %get-tuple-element.32), channel_id=1, source_target_pairs={{0,16},{16,0},{1,17},{17,1},{2,18},{18,2},{3,19},{19,3},{4,20},{20... | collective-permute-start | bytes 663560 | tf_op jit(solution)/shard_map/ppermute | solution.py:140
  13.8 2.1 %shard_map.85 = bf16[4,104,896]{2,1,0:T(8,128)(2,1)} custom-call(bf16[1,104,3328]{2,1,0:T(8,128)(2,1)} %delta_hbm.1), custom_call_target="tpu_custom_call" | custom-call | tf_op jit(solution)/shard_map/pallas_call | solution.py:168
  15.9 4.0 %all-to-all-start = ((bf16[4,104,896]{2,1,0:T(8,128)(2,1)}), bf16[4,104,896]{2,1,0:T(8,128)(2,1)S(1)}, u32[]{:S(2)}, u32[]{:S(2)}) async-start(bf16[4,104,896]{2,1,0:T(8,128)(2,1)} %shard_map.85), calls=%async_computation | async-start | bytes 1490944 | tf_op jit(solution)/shard_map/all_to_all | solution.py:255
  19.9 0.0 all-gather.3.cloned.1.call-start
  19.9 0.1 pad_add_fusion.place_ref
  20.0 0.0 collective-permute-done
  20.0 0.8 pad_maximum_fusion
  20.8 0.9 convert_element_type.4.anchor_ref
  21.7 0.0 all-gather.3.cloned.1.call-update
  21.7 0.9 broadcast_multiply_fusion.stale_ref
  22.6 5.4 %all-to-all-done.sums_ref = bf16[4,104,896]{2,1,0:T(8,128)(2,1)S(1)} async-done(((bf16[4,104,896]{2,1,0:T(8,128)(2,1)}), bf16[4,104,896]{2,1,0:T(8,128)(2,1)S(1)}, u32[]{:S(2)}, u32[]{:S(2)}) %all-to-all-start) | async-done | bytes 745504 | tf_op jit(solution)/shard_map/all_to_all | solution.py:255
  28.1 0.0 copy-start.2
  28.1 0.8 shard_map.86
  28.9 0.0 copy-start
  28.9 0.0 copy-start.1
  28.9 23.1 %all_to_all.20.mixed_ref = bf16[4,2,104,208]{3,2,1,0:T(8,128)(2,1)S(1)} all-to-all(bf16[4,2,104,208]{3,2,1,0:T(8,128)(2,1)S(1)} %shard_map.86), channel_id=1, replica_groups=mesh['x'=4,'zh'=4,'zl'=2,'y'=8,'c'=2] {'zh'}, dimensions={0} | all-to-all | bytes 692224 | tf_op jit(solution)/shard_map/all_to_all | solution.py:258
  52.0 0.3 shard_map.87
  52.3 10.6 %all_to_all.21.blocks_ref = bf16[4,104,896]{2,1,0:T(8,128)(2,1)S(1)} all-to-all(bf16[4,104,896]{2,1,0:T(8,128)(2,1)S(1)} %get-tuple-element.22), channel_id=1, replica_groups=mesh['x'=4,'zh'=4,'zl'=2,'y'=8,'c'=2] {'x'}, dimensions={0} | all-to-all | bytes 1490944 | tf_op jit(solution)/shard_map/all_to_all | solution.py:262
  62.9 0.8 shard_map.88
  63.7 17.1 %all-to-all-start.3 = ((f32[128,1,128]{2,1,0:T(1,128)}), f32[128,1,128]{2,1,0:T(1,128)S(1)}, u32[]{:S(2)}, u32[]{:S(2)}) async-start(f32[128,1,128]{2,1,0:T(1,128)} %get-tuple-element.23), calls=%async_computation.3 | async-start | bytes 131072 | tf_op jit(solution)/shard_map/all_to_all | solution.py:266
  80.8 0.0 all-gather.3.cloned.1.call-done
  80.8 0.0 copy-done.2
  80.8 12.5 %shard_map.89 = bf16[104,3328]{1,0:T(8,128)(2,1)} custom-call(s32[2]{0:T(128)S(1)} %pad_add_fusion.place_ref, bf16[104,3328]{1,0:T(8,128)(2,1)S(1)} %get-tuple-element.24.anchor_ref, bf16[2,104,1024]{2,1,0:T(8,128)(2,1)S(1)} %bitcast.13, bf16[16,2,32,3456]{3,2,1,0:T(8,128)(2,1)} %bitcast.16), custom_call_target="tpu_custom_call" | custom-call | flops 2835349504 | bytes 9000000 | tf_op jit(solution)/shard_map/pallas_call | solution.py:114
  93.4 0.0 all-to-all-done.3.spread_ref
  93.4 0.0 copy-done
  93.4 0.0 copy-done.1
  93.4 0.9 shard_map.90
Async XLA Ops:
  8.9 11.1 %collective-permute-start = (bf16[32,3456]{1,0:T(8,128)(2,1)S(1)}, bf16[32,3456]{1,0:T(8,128)(2,1)S(1)}, u32[]{:S(2)}, u32[]{:S(2)}) collective-permute-start(bf16[32,3456]{1,0:T(8,128)(2,1)S(1)} %get-tuple-element.32), channel_id=1, source_target_pairs={{0,16},{16,0},{1,17},{17,1},{2,18},{18,2},{3,19},{19,3},{4,20},{20... | collective-permute-start | bytes 663560 | tf_op jit(solution)/shard_map/ppermute | solution.py:140
  15.9 12.2 %all-to-all-start = ((bf16[4,104,896]{2,1,0:T(8,128)(2,1)}), bf16[4,104,896]{2,1,0:T(8,128)(2,1)S(1)}, u32[]{:S(2)}, u32[]{:S(2)}) async-start(bf16[4,104,896]{2,1,0:T(8,128)(2,1)} %shard_map.85), calls=%async_computation | async-start | bytes 1490944 | tf_op jit(solution)/shard_map/all_to_all | solution.py:255
  19.9 60.9 %all-gather.3.cloned.1.call-start = ((), (), s32[]{:S(2)}) async-start(), calls=%async_computation.4 | async-start | bytes 7520256 | tf_op jit(solution)/shard_map/all_gather | solution.py:251
  28.1 52.8 %copy-start.2 = (bf16[1,2,104,1024]{3,2,1,0:T(8,128)(2,1)S(1)}, bf16[1,2,104,1024]{3,2,1,0:T(8,128)(2,1)}, u32[]{:S(2)}) copy-start(bf16[1,2,104,1024]{3,2,1,0:T(8,128)(2,1)} %param.11) | copy-start | bytes 1277956
  28.9 64.5 %copy-start = (f32[104,208]{1,0:T(8,128)S(1)}, f32[104,208]{1,0:T(8,128)}, u32[]{:S(2)}) copy-start(f32[104,208]{1,0:T(8,128)} %anchor_ref.1) | copy-start | bytes 259588
  28.9 64.5 %copy-start.1 = (f32[104,208]{1,0:T(8,128)S(1)}, f32[104,208]{1,0:T(8,128)}, u32[]{:S(2)}) copy-start(f32[104,208]{1,0:T(8,128)} %momentum_ref.1) | copy-start | bytes 259588
  63.7 29.7 %all-to-all-start.3 = ((f32[128,1,128]{2,1,0:T(1,128)}), f32[128,1,128]{2,1,0:T(1,128)S(1)}, u32[]{:S(2)}, u32[]{:S(2)}) async-start(f32[128,1,128]{2,1,0:T(1,128)} %get-tuple-element.23), calls=%async_computation.3 | async-start | bytes 131072 | tf_op jit(solution)/shard_map/all_to_all | solution.py:266
Sparse Core Ops, SparseCore 0:
  23.4 57.2 all-gather.2
